TPU v7x, 512 devices: a whole 4x4x16 slice. The times are simulated.
512 devices in a mesh: row: 128 (over y, z, core), col: 4 (over x).
Axes of the slice: x: 4, y: 4, z: 16, core: 2. Of those that a mesh axis runs over, the one named last changes fastest.
Arguments:
- blocks: bfloat16 [1024, 5, 256, 256], P('row', None, 'col'), may hold values from -0.15625 to 0.15625
- samples: bfloat16 [1024, 256, 256], P('row', 'col'), may hold values from -6 to 6
- probes: bfloat16 [1024, 256, 256], P('row', 'col'), may hold values from -6 to 6
- compress: float32 [256, 128], replicated, may hold values from -0.375 to 0.375
- pattern: int32 [1024, 5], P('row'), may hold values from -8 to 1031, as said below
- ranks: int32 [6], replicated, may hold values from 32 to 128
Outputs:
- leaf_bases: bfloat16 [2, 1024, 256, 128], P(None, ('row', 'col'))
- transfers: bfloat16 [2, 512, 5, 256, 128], P(None, ('row', 'col'))
Inputs may be any that keep to these rules, and one draw needn't show every extreme that they name: `pattern`: block row i names column blocks i - 8, i - o, i, i + p, i + 8 in that order, with o and p from 1 to 7.
All inputs are finite; a program needn't handle non-finite values.
Results may differ from a plain program's by a relative error of at most 0.001.
Values may be sent and summed in bfloat16 or wider, within the bound.
A program may use at most 64 MiB of HBM per device.

v0:
```python
import math

import jax
import jax.numpy as jnp
from jax import lax
from jax.sharding import PartitionSpec as P

ROW_LEVELS = 3


def padded(value, sides, width):
    for axis, dim in sides:
        size, length = (lax.axis_size(axis), value.shape[dim])
        up = [(i, (i + 1) % size) for i in range(size - 1)]
        down = [(j, i) for i, j in up]
        last = lax.slice_in_dim(value, length - width, length, axis=dim)
        initial = lax.slice_in_dim(value, 0, width, axis=dim)
        before = lax.ppermute(last, axis, up)
        after = lax.ppermute(initial, axis, down)
        value = jnp.concatenate([before, value, after], axis=dim)
    return value


def passed_along(value, axis, by):
    size = lax.axis_size(axis)
    pairs = [(i, i + by) for i in range(size) if 0 <= i + by < size]
    return lax.ppermute(value, axis, pairs)


def partner(value, axis, distance):
    return lax.ppermute(value, axis, [(i, i ^ 1 << distance) for i in range(lax.axis_size(axis))])


def leaf_factor(sketch, compress):
    hp = lax.Precision.HIGHEST
    wide = jnp.einsum("...bs,sk->...bk", sketch, compress, precision=hp)
    gram = jnp.einsum("...bk,...bj->...kj", wide, wide, precision=hp)
    factor = jnp.linalg.cholesky(gram)
    unit = lax.linalg.triangular_solve(factor, wide, left_side=False, lower=True, transpose_a=True)
    return (factor, unit)


def merge_factor(lower_node, upper_node):
    hp = lax.Precision.HIGHEST
    gram = jnp.einsum("...ik,...jk->...ij", lower_node, lower_node, precision=hp)
    gram = gram + jnp.einsum("...ik,...jk->...ij", upper_node, upper_node, precision=hp)
    return jnp.linalg.cholesky(gram)


def combine(lower_node, upper_node):
    stacked = jnp.concatenate(
        [jnp.swapaxes(lower_node, -1, -2), jnp.swapaxes(upper_node, -1, -2)], axis=-2
    )
    factor = merge_factor(lower_node, upper_node)
    basis = lax.linalg.triangular_solve(
        factor, stacked, left_side=False, lower=True, transpose_a=True
    )
    return (factor, basis)


def order_pair(current, other, upper_side):
    lower_node = jnp.where(upper_side, other, current)
    upper_node = jnp.where(upper_side, current, other)
    return (lower_node, upper_node)


def body(blocks, samples, probes, compress, pattern, ranks):
    row_index = lax.axis_index("row")
    col_index = lax.axis_index("col")
    n_blocks = blocks.shape[0]
    n_slots = blocks.shape[1]
    rows_block = blocks.shape[3]
    n_samples = samples.shape[2]
    rank_max = compress.shape[1]
    local_index = pattern - row_index * n_blocks + n_blocks
    full_rows = lax.all_gather(samples, "col", axis=1, tiled=True)
    extended = padded(full_rows, (("row", 0),), n_blocks)
    partial_value = jnp.zeros((n_blocks, blocks.shape[2], n_samples), jnp.float32)
    for slot in range(n_slots):
        picked = extended[local_index[:, slot]]
        partial_value = partial_value + jnp.einsum(
            "nrc,ncs->nrs", blocks[:, slot], picked, preferred_element_type=jnp.float32
        )
    row_sketch = lax.all_to_all(partial_value, "col", split_axis=0, concat_axis=1, tiled=True)
    buffer = jnp.zeros((3 * n_blocks, rows_block, n_samples), jnp.float32)
    for slot in range(n_slots):
        term = jnp.einsum(
            "nrc,nrs->ncs", blocks[:, slot], probes, preferred_element_type=jnp.float32
        )
        buffer = buffer.at[local_index[:, slot]].add(term)
    from_above = passed_along(buffer[:n_blocks], "row", -1)
    from_below = passed_along(buffer[2 * n_blocks :], "row", 1)
    adjoint_part = buffer[n_blocks : 2 * n_blocks] + from_above + from_below
    col_sketch = lax.psum_scatter(adjoint_part, "col", scatter_dimension=0, tiled=True)
    sides = jnp.stack([row_sketch, col_sketch])
    factor, unit = leaf_factor(sides, compress)
    columns = jnp.arange(rank_max, dtype=jnp.int32)
    leaf_mask = (columns < ranks[0]).astype(jnp.float32)
    leaf_bases = (unit * math.sqrt(rows_block) * leaf_mask).astype(jnp.bfloat16)
    current = factor
    while current.shape[1] > 1:
        count = current.shape[1] // 2
        paired = current.reshape(2, count, 2, rank_max, rank_max)
        current = merge_factor(paired[:, :, 0], paired[:, :, 1])
    current = current[:, 0]
    collected = []
    col_bits = lax.axis_size("col").bit_length() - 1
    for bit in range(col_bits):
        other = partner(current, "col", bit)
        upper_side = col_index >> bit & 1 == 1
        lower_node, upper_node = order_pair(current, other, upper_side)
        current, basis = combine(lower_node, upper_node)
        collected.append(basis)
    for bit in range(ROW_LEVELS):
        other = partner(current, "row", bit)
        upper_side = row_index >> bit & 1 == 1
        lower_node, upper_node = order_pair(current, other, upper_side)
        current, basis = combine(lower_node, upper_node)
        collected.append(basis)
    stacked = jnp.stack(collected, axis=1)
    level_mask = (columns[None, :] < ranks[1:][:, None]).astype(jnp.float32)
    scaled = stacked * math.sqrt(2 * rank_max) * level_mask[None, :, None, :]
    transfers = scaled[:, None].astype(jnp.bfloat16)
    return (leaf_bases, transfers)


def solution(mesh):
    return jax.shard_map(
        body,
        mesh=mesh,
        in_specs=(
            P("row", None, "col", None),
            P("row", "col", None),
            P("row", "col", None),
            P(),
            P("row", None),
            P(),
        ),
        out_specs=(P(None, ("row", "col"), None, None), P(None, ("row", "col"), None, None, None)),
        check_vma=False,
    )
```

profile of v0, /device:TPU:1, one launch (start us, length us, event | category | flops | bytes accessed | tf_op | source)
XLA Modules:
  0.0 506.1 jit_solution(2643835121193211553)
XLA Ops:
  7.2 0.9 copy-done
  8.1 2.8 fusion.46
  10.9 1.8 fusion.42
  12.7 1.9 fusion.38
  14.6 1.8 fusion.34
  16.4 1.4 fusion.30
  18.1 3.4 broadcast_in_dim.10
  21.5 5.1 %scatter_fusion = f32[24,256,256]{2,1,0:T(8,128)} fusion(f32[24,256,256]{2,1,0:T(8,128)} %broadcast_in_dim.10, s32[8]{0:T(128)S(1)} %get-tuple-element.12, f32[8,256,256]{2,1,0:T(8,128)} %fusion.46), kind=kCustom, calls=%fused_computation.5 | custom fusion | flops 524288 | bytes 6291488 | tf_op jit(solution)/shard_map/scatter-add | solution.py:90
  26.6 4.8 scatter_fusion.1
  31.5 5.1 %scatter_fusion.2 = f32[24,256,256]{2,1,0:T(8,128)} fusion(f32[24,256,256]{2,1,0:T(8,128)} %scatter_fusion.1, s32[8]{0:T(128)S(1)} %get-tuple-element.10, f32[8,256,256]{2,1,0:T(8,128)} %fusion.38), kind=kCustom, calls=%fused_computation.7 | custom fusion | flops 524288 | bytes 6291488 | tf_op jit(solution)/shard_map/scatter-add | solution.py:90
  36.6 4.9 scatter_fusion.3
  41.5 4.4 scatter_fusion.4
  45.9 4.6 fusion.102
  50.5 8.9 %collective-permute-start.2 = (f32[8,256,256]{2,1,0:T(8,128)}, f32[8,256,256]{2,1,0:T(8,128)S(1)}, u32[]{:S(2)}, u32[]{:S(2)}) collective-permute-start(f32[8,256,256]{2,1,0:T(8,128)} %get-tuple-element.21), channel_id=1, source_target_pairs={{4,0},{8,4},{12,8},{16,12},{20,16},{24,20},{28,24},{32,28},{36,32}... | collective-permute-start | bytes 6291464 | tf_op jit(solution)/shard_map/ppermute | solution.py:27
  59.4 1.9 collective-permute-start.3
  61.4 18.1 %collective-permute-done.2 = f32[8,256,256]{2,1,0:T(8,128)S(1)} collective-permute-done((f32[8,256,256]{2,1,0:T(8,128)}, f32[8,256,256]{2,1,0:T(8,128)S(1)}, u32[]{:S(2)}, u32[]{:S(2)}) %collective-permute-start.2) | collective-permute-done | bytes 2097184 | tf_op jit(solution)/shard_map/ppermute | solution.py:27
  79.5 5.1 %collective-permute-done.3 = f32[8,256,256]{2,1,0:T(8,128)} collective-permute-done((f32[8,256,256]{2,1,0:T(8,128)}, f32[8,256,256]{2,1,0:T(8,128)}, u32[]{:S(2)}, u32[]{:S(2)}) %collective-permute-start.3) | collective-permute-done | bytes 2097184 | tf_op jit(solution)/shard_map/ppermute | solution.py:27
  84.6 4.0 fusion
  88.6 3.5 all-gather.2.cloned.1.call-done
  92.1 4.6 collective-permute-start
  96.8 1.9 collective-permute-start.1
  98.9 9.9 %collective-permute-done = bf16[8,256,256]{2,1,0:T(8,128)(2,1)} collective-permute-done((bf16[8,256,256]{2,1,0:T(8,128)(2,1)}, bf16[8,256,256]{2,1,0:T(8,128)(2,1)}, u32[]{:S(2)}, u32[]{:S(2)}) %collective-permute-start) | collective-permute-done | bytes 1048608 | tf_op jit(solution)/shard_map/ppermute | solution.py:18
  108.8 1.3 constant_dynamic-update-slice_fusion.2
  110.2 3.0 collective-permute-done.1
  113.2 1.3 constant_dynamic-update-slice_fusion
  114.5 1.6 gather_fusion.4
  116.1 1.6 gather_fusion.3
  117.8 1.6 gather_fusion.2
  119.4 1.6 gather_fusion.1
  121.0 1.6 gather_fusion
  122.6 1.7 fusion.32
  124.3 1.7 fusion.36
  126.7 0.6 copy-done.5
  127.3 1.1 fusion.4
  128.4 3.6 all-to-all-start
  132.2 6.7 %all-to-all-done = f32[8,64,256]{2,1,0:T(8,128)S(1)} async-done(((f32[8,64,256]{2,1,0:T(8,128)}), f32[8,64,256]{2,1,0:T(8,128)S(1)}, u32[]{:S(2)}, u32[]{:S(2)}) %all-to-all-start) | async-done | bytes 524320 | tf_op jit(solution)/shard_map/all_to_all | solution.py:84
  139.0 2.0 fusion.11
  141.1 1.1 fusion.103
  142.3 46.9 %custom-call.17 = f32[2,2,128,128]{3,2,1,0:T(8,128)S(1)} custom-call(f32[2,2,128,128]{3,2,1,0:T(8,128)S(1)} %fusion.50), custom_call_target="Cholesky" | custom-call | tf_op jit(solution)/shard_map/jit(cholesky)/cholesky | solution.py:38
  190.4 23.5 %custom-call.19 = f32[2,1,128,128]{3,2,1,0:T(8,128)S(1)} custom-call(f32[2,1,128,128]{3,2,1,0:T(8,128)S(1)} %fusion.63), custom_call_target="Cholesky" | custom-call | tf_op jit(solution)/shard_map/jit(cholesky)/cholesky | solution.py:47
  214.2 2.4 collective-permute-start.4
  216.6 39.3 %custom-call.18 = f32[2,2,1,128,128]{3,4,2,1,0:T(8,128)S(1)} custom-call(f32[2,2,1,128,128]{4,3,2,1,0:T(8,128)S(1)} %get-tuple-element.24), custom_call_target="InvertDiagBlocksLowerTriangular" | custom-call | tf_op jit(solution)/shard_map/triangular_solve | solution.py:39
  255.9 1.3 fusion.5
  258.2 23.5 %custom-call.28 = f32[2,128,128]{2,1,0:T(8,128)S(1)} custom-call(f32[2,128,128]{2,1,0:T(8,128)S(1)} %fusion.74), custom_call_target="Cholesky" | custom-call | tf_op jit(solution)/shard_map/jit(cholesky)/cholesky | solution.py:47
  281.9 3.9 collective-permute-start.5
  285.8 19.7 %custom-call.29 = f32[2,1,128,128]{2,3,1,0:T(8,128)S(1)} custom-call(f32[2,1,128,128]{3,2,1,0:T(8,128)S(1)} %get-tuple-element.19), custom_call_target="InvertDiagBlocksLowerTriangular" | custom-call | tf_op jit(solution)/shard_map/triangular_solve/custom-call.4 | solution.py:55
  305.6 0.4 fusion.10
  307.0 23.5 %custom-call.30 = f32[2,128,128]{2,1,0:T(8,128)S(1)} custom-call(f32[2,128,128]{2,1,0:T(8,128)S(1)} %fusion.72), custom_call_target="Cholesky" | custom-call | tf_op jit(solution)/shard_map/jit(cholesky)/cholesky | solution.py:47
  330.7 2.4 collective-permute-start.6
  333.1 19.7 %custom-call.31 = f32[2,1,128,128]{2,3,1,0:T(8,128)S(1)} custom-call(f32[2,1,128,128]{3,2,1,0:T(8,128)S(1)} %get-tuple-element.17), custom_call_target="InvertDiagBlocksLowerTriangular" | custom-call | tf_op jit(solution)/shard_map/triangular_solve/custom-call.4 | solution.py:55
  352.8 0.4 fusion.9
  354.2 23.5 %custom-call.32 = f32[2,128,128]{2,1,0:T(8,128)S(1)} custom-call(f32[2,128,128]{2,1,0:T(8,128)S(1)} %fusion.70), custom_call_target="Cholesky" | custom-call | tf_op jit(solution)/shard_map/jit(cholesky)/cholesky | solution.py:47
  377.9 5.7 %collective-permute-start.7 = (f32[2,128,128]{2,1,0:T(8,128)S(1)}, f32[2,128,128]{2,1,0:T(8,128)S(1)}, u32[]{:S(2)}, u32[]{:S(2)}) collective-permute-start(f32[2,128,128]{2,1,0:T(8,128)S(1)} %get-tuple-element.16), channel_id=1, source_target_pairs={{0,8},{4,12},{8,0},{12,4},{16,24},{20,28},{24,16},{28,20},{32,40},... | collective-permute-start | bytes 393224 | tf_op jit(solution)/shard_map/ppermute | solution.py:31
  383.6 19.7 %custom-call.33 = f32[2,1,128,128]{2,3,1,0:T(8,128)S(1)} custom-call(f32[2,1,128,128]{3,2,1,0:T(8,128)S(1)} %get-tuple-element.15), custom_call_target="InvertDiagBlocksLowerTriangular" | custom-call | tf_op jit(solution)/shard_map/triangular_solve/custom-call.4 | solution.py:55
  403.3 0.4 fusion.8
  404.7 23.5 %custom-call.34 = f32[2,128,128]{2,1,0:T(8,128)S(1)} custom-call(f32[2,128,128]{2,1,0:T(8,128)S(1)} %fusion.68), custom_call_target="Cholesky" | custom-call | tf_op jit(solution)/shard_map/jit(cholesky)/cholesky | solution.py:47
  428.4 4.4 collective-permute-start.8
  432.8 19.7 %custom-call.35 = f32[2,1,128,128]{2,3,1,0:T(8,128)S(1)} custom-call(f32[2,1,128,128]{3,2,1,0:T(8,128)S(1)} %get-tuple-element.13), custom_call_target="InvertDiagBlocksLowerTriangular" | custom-call | tf_op jit(solution)/shard_map/triangular_solve/custom-call.4 | solution.py:55
  452.5 0.4 fusion.7
  453.4 0.4 convolution_add_fusion.1
  453.9 23.5 %custom-call.36 = f32[2,128,128]{2,1,0:T(8,128)S(1)} custom-call(f32[2,128,128]{2,1,0:T(8,128)S(1)} %fusion.66), custom_call_target="Cholesky" | custom-call | tf_op jit(solution)/shard_map/jit(cholesky)/cholesky | solution.py:47
  477.6 19.7 %custom-call.37 = f32[2,1,128,128]{2,3,1,0:T(8,128)S(1)} custom-call(f32[2,1,128,128]{3,2,1,0:T(8,128)S(1)} %select_bitcast_fusion.1), custom_call_target="InvertDiagBlocksLowerTriangular" | custom-call | tf_op jit(solution)/shard_map/triangular_solve/custom-call.4 | solution.py:55
  497.3 0.4 fusion.6
  497.9 1.1 copy.83
  (94 shorter events, 8.7 us)
Async XLA Ops:
  7.2 1.0 copy-start
  7.2 3.7 copy-start.1
  7.2 84.9 %all-gather.2.cloned.1.call-start = ((), (), s32[]{:S(2)}) async-start(), calls=%async_computation.2 | async-start | bytes 1310720 | tf_op jit(solution)/shard_map/all_gather | solution.py:76
  14.6 3.3 copy-start.8
  50.5 29.0 %collective-permute-start.2 = (f32[8,256,256]{2,1,0:T(8,128)}, f32[8,256,256]{2,1,0:T(8,128)S(1)}, u32[]{:S(2)}, u32[]{:S(2)}) collective-permute-start(f32[8,256,256]{2,1,0:T(8,128)} %get-tuple-element.21), channel_id=1, source_target_pairs={{4,0},{8,4},{12,8},{16,12},{20,16},{24,20},{28,24},{32,28},{36,32}... | collective-permute-start | bytes 6291464 | tf_op jit(solution)/shard_map/ppermute | solution.py:27
  59.4 25.2 %collective-permute-start.3 = (f32[8,256,256]{2,1,0:T(8,128)}, f32[8,256,256]{2,1,0:T(8,128)}, u32[]{:S(2)}, u32[]{:S(2)}) collective-permute-start(f32[8,256,256]{2,1,0:T(8,128)} %get-tuple-element.22), channel_id=1, source_target_pairs={{0,4},{4,8},{8,12},{12,16},{16,20},{20,24},{24,28},{28,32},{32,36}... | collective-permute-start | bytes 6291464 | tf_op jit(solution)/shard_map/ppermute | solution.py:27
  61.4 77.7 %reduce-scatter.2.cloned.1.call-start = ((), (), s32[]{:S(2)}) async-start(), calls=%async_computation.3 | async-start | bytes 2621440 | tf_op jit(solution)/shard_map/reduce_scatter | solution.py:94
  88.6 10.1 %copy-start.9 = (s32[6]{0:T(128)S(1)}, s32[6]{0:T(128)}, u32[]{:S(2)}) copy-start(s32[6]{0:T(128)} %param.14) | copy-start | bytes 76
  92.1 16.7 %collective-permute-start = (bf16[8,256,256]{2,1,0:T(8,128)(2,1)}, bf16[8,256,256]{2,1,0:T(8,128)(2,1)}, u32[]{:S(2)}, u32[]{:S(2)}) collective-permute-start(bf16[8,256,256]{2,1,0:T(8,128)(2,1)} %all-gather.2.cloned.1.call-done), channel_id=1, source_target_pairs={{0,4},{4,8},{8,12},{12,16},{16,20},{20,24},{24,28},{28,32},{32,36}... | collective-permute-start | bytes 3145736 | tf_op jit(solution)/shard_map/ppermute | solution.py:18
  96.8 16.4 %collective-permute-start.1 = (bf16[8,256,256]{2,1,0:T(8,128)(2,1)}, bf16[8,256,256]{2,1,0:T(8,128)(2,1)}, u32[]{:S(2)}, u32[]{:S(2)}) collective-permute-start(bf16[8,256,256]{2,1,0:T(8,128)(2,1)} %all-gather.2.cloned.1.call-done), channel_id=1, source_target_pairs={{4,0},{8,4},{12,8},{16,12},{20,16},{24,20},{28,24},{32,28},{36,32}... | collective-permute-start | bytes 3145736 | tf_op jit(solution)/shard_map/ppermute | solution.py:19
  98.7 11.4 %copy-start.6 = (bf16[8,256,256]{2,1,0:T(8,128)(2,1)S(1)}, bf16[8,256,256]{2,1,0:T(8,128)(2,1)}, u32[]{:S(2)}) copy-start(bf16[8,256,256]{2,1,0:T(8,128)(2,1)} %all-gather.2.cloned.1.call-done) | copy-start | bytes 3145732
  122.6 3.5 copy-start.2
  122.6 3.5 copy-start.3
  124.3 2.1 copy-start.4
  126.1 1.2 copy-start.5
  127.3 11.7 %copy-start.7 = (f32[256,128]{1,0:T(8,128)S(1)}, f32[256,128]{1,0:T(8,128)}, u32[]{:S(2)}) copy-start(f32[256,128]{1,0:T(8,128)} %param.12) | copy-start | bytes 393220
  128.4 10.5 %all-to-all-start = ((f32[8,64,256]{2,1,0:T(8,128)}), f32[8,64,256]{2,1,0:T(8,128)S(1)}, u32[]{:S(2)}, u32[]{:S(2)}) async-start(f32[8,64,256]{2,1,0:T(8,128)} %fusion.4), calls=%async_computation | async-start | bytes 1048576 | tf_op jit(solution)/shard_map/all_to_all | solution.py:84
  214.2 43.1 %collective-permute-start.4 = (f32[2,128,128]{2,1,0:T(8,128)S(1)}, f32[2,128,128]{2,1,0:T(8,128)S(1)}, u32[]{:S(2)}, u32[]{:S(2)}) collective-permute-start(f32[2,128,128]{2,1,0:T(8,128)S(1)} %select_bitcast_fusion.6), channel_id=1, source_target_pairs={{0,1},{1,0},{2,3},{3,2},{4,5},{5,4},{6,7},{7,6},{8,9},{9,8},{10,11... | collective-permute-start | bytes 393224 | tf_op jit(solution)/shard_map/ppermute | solution.py:31
  281.9 24.2 %collective-permute-start.5 = (f32[2,128,128]{2,1,0:T(8,128)S(1)}, f32[2,128,128]{2,1,0:T(8,128)S(1)}, u32[]{:S(2)}, u32[]{:S(2)}) collective-permute-start(f32[2,128,128]{2,1,0:T(8,128)S(1)} %get-tuple-element.20), channel_id=1, source_target_pairs={{0,2},{1,3},{2,0},{3,1},{4,6},{5,7},{6,4},{7,5},{8,10},{9,11},{10,... | collective-permute-start | bytes 393224 | tf_op jit(solution)/shard_map/ppermute | solution.py:31
  330.7 22.5 %collective-permute-start.6 = (f32[2,128,128]{2,1,0:T(8,128)S(1)}, f32[2,128,128]{2,1,0:T(8,128)S(1)}, u32[]{:S(2)}, u32[]{:S(2)}) collective-permute-start(f32[2,128,128]{2,1,0:T(8,128)S(1)} %get-tuple-element.18), channel_id=1, source_target_pairs={{0,4},{4,0},{8,12},{12,8},{16,20},{20,16},{24,28},{28,24},{32,36},... | collective-permute-start | bytes 393224 | tf_op jit(solution)/shard_map/ppermute | solution.py:31
  377.9 25.8 %collective-permute-start.7 = (f32[2,128,128]{2,1,0:T(8,128)S(1)}, f32[2,128,128]{2,1,0:T(8,128)S(1)}, u32[]{:S(2)}, u32[]{:S(2)}) collective-permute-start(f32[2,128,128]{2,1,0:T(8,128)S(1)} %get-tuple-element.16), channel_id=1, source_target_pairs={{0,8},{4,12},{8,0},{12,4},{16,24},{20,28},{24,16},{28,20},{32,40},... | collective-permute-start | bytes 393224 | tf_op jit(solution)/shard_map/ppermute | solution.py:31
  428.4 24.6 %collective-permute-start.8 = (f32[2,128,128]{2,1,0:T(8,128)S(1)}, f32[2,128,128]{2,1,0:T(8,128)S(1)}, u32[]{:S(2)}, u32[]{:S(2)}) collective-permute-start(f32[2,128,128]{2,1,0:T(8,128)S(1)} %get-tuple-element.14), channel_id=1, source_target_pairs={{0,16},{4,20},{8,24},{12,28},{16,0},{20,4},{24,8},{28,12},{32,48},... | collective-permute-start | bytes 393224 | tf_op jit(solution)/shard_map/ppermute | solution.py:31
Sparse Core Ops, SparseCore 0:
  61.5 30.6 all-gather.1
  95.0 41.4 reduce-scatter.1
where the time goes:
time: 514 us; the launch traced here: 506 us
  other arithmetic  356 us (69%)
  waiting for transfers between devices  46.5 us (9%)
  starting transfers between devices  40 us (8%)
  matrix products  26.1 us (5%)
  local copies, waits for them, and re-layouts  22.1 us (4%)
  between operations  15 us (3%)
    another operation x18, other arithmetic, merge_factor(): return jnp.linalg.cholesky(gram)  142 us
    another operation x10, other arithmetic, combine(): lax.linalg.triangular_solve(factor, stacked, left_side=False, lower=True,...  98.9 us
    another operation x4, other arithmetic, leaf_factor(): factor = jnp.linalg.cholesky(gram)  47.1 us
    another operation x2, other arithmetic, leaf_factor(): lax.linalg.triangular_solve(factor, wide, left_side=False, lower=True, tr...  39.3 us
    scatter-add x5, other arithmetic, body(): buffer = buffer.at[local_index[:, slot]].add(term)  24.4 us
    ppermute x2, waiting for transfers between devices, passed_along(): return lax.ppermute(value, axis, pairs)  23.2 us
    ppermute x5, starting transfers between devices, partner(): lax.ppermute(value, axis, [(i, i ^ 1 << distance) for i in range(lax.axis...  18.9 us
    ppermute x2, starting transfers between devices, passed_along(): return lax.ppermute(value, axis, pairs)  10.8 us
  transfers between devices with their start and end apart: 12, of which 6 were waited for; matrix products, arithmetic and copies ran while one was open for 28% of the time, Pallas kernels for 0%

commit v1 on v0

v1 whole, which is shorter than its diff:
```python
import math

import jax
import jax.numpy as jnp
from jax import lax
from jax.experimental import pallas as pl
from jax.experimental.pallas import tpu as pltpu
from jax.sharding import PartitionSpec as P

ROW_LEVELS = 3


def padded(value, sides, width):
    for axis, dim in sides:
        size, length = (lax.axis_size(axis), value.shape[dim])
        up = [(i, (i + 1) % size) for i in range(size - 1)]
        down = [(j, i) for i, j in up]
        last = lax.slice_in_dim(value, length - width, length, axis=dim)
        initial = lax.slice_in_dim(value, 0, width, axis=dim)
        before = lax.ppermute(last, axis, up)
        after = lax.ppermute(initial, axis, down)
        value = jnp.concatenate([before, value, after], axis=dim)
    return value


def passed_along(value, axis, by):
    size = lax.axis_size(axis)
    pairs = [(i, i + by) for i in range(size) if 0 <= i + by < size]
    return lax.ppermute(value, axis, pairs)


def partner(value, axis, distance):
    return lax.ppermute(value, axis, [(i, i ^ 1 << distance) for i in range(lax.axis_size(axis))])


K = 128
F32 = jnp.float32
BF16 = jnp.bfloat16

def pieces(x):
    h = x.astype(BF16).astype(F32)
    r = x - h
    m = r.astype(BF16).astype(F32)
    return h, m, r - m

def panel(S, E, g, p, with_e):
    base = (g * 16 + p) * 64
    rows = [S[pl.ds(base + r, 8, stride=8), :] for r in range(8)]
    erows = [E[pl.ds(base + r, 8, stride=8), :] for r in range(8)] if with_e else None
    a = {}
    for r in range(8):
        for k in range(r, 8):
            c = 8 * p + k
            a[r, k] = jnp.broadcast_to(rows[r][:, c:c + 1], (8, K))
    for r in range(8):
        inv = lax.rsqrt(a[r, r])
        u = {k: a[r, k] * inv for k in range(r + 1, 8)}
        rows[r] = rows[r] * inv
        if with_e:
            erows[r] = erows[r] * inv
        for i in range(r + 1, 8):
            for k in range(i, 8):
                a[i, k] = a[i, k] - u[i] * u[k]
            rows[i] = rows[i] - u[i] * rows[r]
            if with_e:
                erows[i] = erows[i] - u[i] * erows[r]
    for r in range(8):
        S[pl.ds(base + r, 8, stride=8), :] = rows[r]
        if with_e:
            E[pl.ds(base + r, 8, stride=8), :] = erows[r]

def trail(S, E, g, p, b, with_e):
    if p == 15:
        return
    at = lambda q: pl.ds(((g * 16 + q) * 8 + b) * 8, 8)
    h, m, l = pieces(S[at(p), :])
    first = (8 * (p + 1)) // 16 * 16
    left = jnp.concatenate([h, h, h, m, m, l], axis=0).T[first:].astype(BF16)
    right = jnp.concatenate([h, m, l, h, m, h], axis=0)
    if with_e:
        h, m, l = pieces(E[at(p), :])
        right = jnp.concatenate([right, jnp.concatenate([h, m, l, h, m, h], axis=0)], axis=1)
    t = jnp.dot(left, right.astype(BF16), preferred_element_type=F32)
    for q in range(p + 1, 16):
        o = 8 * q - first
        S[at(q), :] = S[at(q), :] - t[o:o + 8, :K]
        if with_e:
            E[at(q), :] = E[at(q), :] - t[o:o + 8, K:]

def get(ref, g, b):
    return jnp.concatenate([ref[pl.ds(((g * 16 + q) * 8 + b) * 8, 8), :] for q in range(16)], axis=0)

def put(ref, g, b, x):
    for q in range(16):
        ref[pl.ds(((g * 16 + q) * 8 + b) * 8, 8), :] = x[8 * q:8 * q + 8]

def cat(x, order):
    h, m, l = x
    d = {"h": h, "m": m, "l": l}
    return jnp.concatenate([d[c] for c in order], axis=1)

def exact_nt(x, y):
    a = cat([v.astype(BF16) for v in pieces(x)], "hhmhml")
    b = cat([v.astype(BF16) for v in pieces(y)], "hmhlmh")
    return lax.dot_general(a, b, (((1,), (1,)), ((), ())), preferred_element_type=F32)

def kernel(bits, ranks, wide, gram, own1, chain, sib, leaf_out, tr_out, S, E):
    eye = (lax.broadcasted_iota(jnp.int32, (K, K), 0) == lax.broadcasted_iota(jnp.int32, (K, K), 1)).astype(F32)
    def place(i, x):
        put(S, i // 8, i % 8, x)
    for s in range(2):
        for l in range(2):
            place(s * 2 + l, gram[s, l])
        for j in range(5):
            place(4 + s * 5 + j, chain[s, j])
            place(18 + s * 5 + j, sib[s, j])
        place(16 + s, own1[s])
    for i in (14, 15, 28, 29, 30, 31):
        place(i, eye)
    for g in range(2):
        for b in range(8):
            put(E, g, b, eye)
    for p in range(16):
        for g in range(4):
            panel(S, E, g, p, g < 2)
        for g in range(4):
            for b in range(8):
                if g * 8 + b in (14, 15, 28, 29, 30, 31):
                    continue
                trail(S, E, g, p, b, g < 2)
    lane = lax.broadcasted_iota(jnp.int32, (K, K), 1)
    X = lambda i: get(E, i // 8, i % 8)
    U = lambda i: jnp.where(lax.broadcasted_iota(jnp.int32, (K, K), 0) <= lane, get(S, i // 8, i % 8), 0.0)
    scale = math.sqrt(256)
    for s in range(2):
        keep = jnp.where(lane < ranks[0], scale, 0.0)
        for l in range(2):
            x = X(s * 2 + l)
            for half in range(2):
                leaf_out[s, l, pl.ds(half * K, K), :] = (exact_nt(wide[s, l, half * K:half * K + K, :], x) * keep).astype(BF16)
        for j in range(5):
            keep = jnp.where(lane < ranks[j + 1], scale, 0.0)
            own = U(16 + s) if j == 0 else U(4 + s * 5 + j - 1)
            other = U(18 + s * 5 + j)
            x = X(4 + s * 5 + j)
            up = bits[j]
            tr_out[s, 0, j, pl.ds(pl.multiple_of(up * K, K), K), :] = (exact_nt(own, x) * keep).astype(BF16)
            tr_out[s, 0, j, pl.ds(pl.multiple_of((1 - up) * K, K), K), :] = (exact_nt(other, x) * keep).astype(BF16)

def finish(bits, ranks, wide, gram, own1, chain, sib):
    vm = pl.BlockSpec(memory_space=pltpu.VMEM)
    sm = pl.BlockSpec(memory_space=pltpu.SMEM)
    return pl.pallas_call(
        kernel,
        out_shape=(jax.ShapeDtypeStruct((2, 2, 256, K), BF16), jax.ShapeDtypeStruct((2, 1, 5, 256, K), BF16)),
        in_specs=[sm, sm, vm, vm, vm, vm, vm],
        out_specs=(vm, vm),
        scratch_shapes=[pltpu.VMEM((4 * 1024, K), F32), pltpu.VMEM((2 * 1024, K), F32)],
        compiler_params=pltpu.CompilerParams(vmem_limit_bytes=48 << 20),
    )(bits, ranks, wide, gram, own1, chain, sib)


def body(blocks, samples, probes, compress, pattern, ranks):
    row_index = lax.axis_index("row")
    col_index = lax.axis_index("col")
    n_blocks = blocks.shape[0]
    n_slots = blocks.shape[1]
    rows_block = blocks.shape[3]
    n_samples = samples.shape[2]
    rank_max = compress.shape[1]
    local_index = pattern - row_index * n_blocks + n_blocks
    full_rows = lax.all_gather(samples, "col", axis=1, tiled=True)
    extended = padded(full_rows, (("row", 0),), n_blocks)
    partial_value = jnp.zeros((n_blocks, blocks.shape[2], n_samples), jnp.float32)
    for slot in range(n_slots):
        picked = extended[local_index[:, slot]]
        partial_value = partial_value + jnp.einsum(
            "nrc,ncs->nrs", blocks[:, slot], picked, preferred_element_type=jnp.float32
        )
    row_sketch = lax.all_to_all(partial_value, "col", split_axis=0, concat_axis=1, tiled=True)
    buffer = jnp.zeros((3 * n_blocks, rows_block, n_samples), jnp.float32)
    for slot in range(n_slots):
        term = jnp.einsum(
            "nrc,nrs->ncs", blocks[:, slot], probes, preferred_element_type=jnp.float32
        )
        buffer = buffer.at[local_index[:, slot]].add(term)
    from_above = passed_along(buffer[:n_blocks], "row", -1)
    from_below = passed_along(buffer[2 * n_blocks :], "row", 1)
    adjoint_part = buffer[n_blocks : 2 * n_blocks] + from_above + from_below
    col_sketch = lax.psum_scatter(adjoint_part, "col", scatter_dimension=0, tiled=True)
    hp = lax.Precision.HIGHEST
    sides = jnp.stack([row_sketch, col_sketch])
    wide = jnp.einsum("...bs,sk->...bk", sides, compress, precision=hp)
    gram = jnp.einsum("...bk,...bj->...kj", wide, wide, precision=hp)
    current = gram[:, 0] + gram[:, 1]
    chain = [current]
    siblings = []
    bits = []
    for axis, index, levels in (("col", col_index, 2), ("row", row_index, ROW_LEVELS)):
        for bit in range(levels):
            other = partner(current, axis, bit)
            current = current + other
            siblings.append(other)
            chain.append(current)
            bits.append(index >> bit & 1)
    return finish(
        jnp.stack(bits), ranks, wide, gram, chain[0], jnp.stack(chain[1:], 1), jnp.stack(siblings, 1)
    )


def solution(mesh):
    return jax.shard_map(
        body,
        mesh=mesh,
        in_specs=(
            P("row", None, "col", None),
            P("row", "col", None),
            P("row", "col", None),
            P(),
            P("row", None),
            P(),
        ),
        out_specs=(P(None, ("row", "col"), None, None), P(None, ("row", "col"), None, None, None)),
        check_vma=False,
    )
```

time: 514 us -> 200 us (0.39); the launches traced: 506 us -> 199 us
  other arithmetic: 356 us -> 28.8 us
  waiting for transfers between devices: 46.5 us -> 61.8 us
  Pallas kernels: 0 us -> 13.5 us
  blocking collectives: 0 us -> 12 us
  matrix products: 26.1 us -> 17.1 us
  starting transfers between devices: 40 us -> 33.7 us
    another operation x34 -> x1, other arithmetic: 327 us -> 0.02 us  [body(): jnp.stack(chain[1:], 1)]
    ppermute x5, waiting for transfers between devices: 0.01 us -> 18.6 us  [partner(): lax.ppermute(value, axis, [(i, i ^ 1 << distance) for i in range(lax.axis...]
    pallas_call x0 -> x1, Pallas kernels: none -> 13.5 us  [finish(): pl.pallas_call(kernel, out_shape=(jax.ShapeDtypeStruct((2, 2, 256, K), BF...]
    all_to_all x0 -> x1, blocking collectives: none -> 12 us  [body(): lax.all_to_all(partial_value, 'col', split_axis=0, concat_axis=1, tiled=T...]
    all_to_all x1 -> x0, waiting for transfers between devices: 6.74 us -> none  [body(): lax.all_to_all(partial_value, 'col', split_axis=0, concat_axis=1, tiled=T...]
  transfers between devices with their start and end apart: 12 -> 11, of which waited for: 6 -> 10; matrix products, arithmetic and copies ran while one was open for 28% -> 8% of each run, Pallas kernels for 0% -> 0%
where the time goes in v1:
time: 200 us; the launch traced here: 199 us
  waiting for transfers between devices  61.8 us (31%)
  starting transfers between devices  33.7 us (17%)
  other arithmetic  28.8 us (14%)
  local copies, waits for them, and re-layouts  18 us (9%)
  matrix products  17.1 us (9%)
  between operations  14.4 us (7%)
  Pallas kernels  13.5 us (7%)
  blocking collectives  12 us (6%)
    scatter-add x5, other arithmetic, body(): buffer = buffer.at[local_index[:, slot]].add(term)  24.5 us
    ppermute x2, waiting for transfers between devices, passed_along(): return lax.ppermute(value, axis, pairs)  22.4 us
    ppermute x5, waiting for transfers between devices, partner(): lax.ppermute(value, axis, [(i, i ^ 1 << distance) for i in range(lax.axis...  18.6 us
    ppermute x5, starting transfers between devices, partner(): lax.ppermute(value, axis, [(i, i ^ 1 << distance) for i in range(lax.axis...  16.7 us
    pallas_call x1, Pallas kernels, finish(): pl.pallas_call(kernel, out_shape=(jax.ShapeDtypeStruct((2, 2, 256, K), BF...  13.5 us
    all_to_all x1, blocking collectives, body(): lax.all_to_all(partial_value, 'col', split_axis=0, concat_axis=1, tiled=T...  12 us
    ppermute x2, starting transfers between devices, passed_along(): return lax.ppermute(value, axis, pairs)  10.2 us
    ppermute x1, waiting for transfers between devices, padded(): before = lax.ppermute(last, axis, up)  10.1 us
  transfers between devices with their start and end apart: 11, of which 10 were waited for; matrix products, arithmetic and copies ran while one was open for 8% of the time, Pallas kernels for 0%

profile of v1, /device:TPU:1, one launch (start us, length us, event | category | flops | bytes accessed | tf_op | source)
XLA Modules:
  0.0 199.4 jit_solution(9626383823848248373)
XLA Ops:
  7.2 0.0 copy-start
  7.2 0.0 copy-start.2
  7.2 0.0 all-gather.2.cloned.1.call-start
  7.2 0.9 copy-done
  8.1 2.8 %fusion.25 = f32[8,256,256]{2,1,0:T(8,128)} fusion(bf16[8,64,256]{2,1,0:T(8,128)(2,1)S(1)} %copy-done, bf16[8,5,64,256]{3,2,1,0:T(8,128)(2,1)} %param.6), kind=kOutput, calls=%fused_computation.37 | convolution fusion | flops 67108864 | bytes 2621440 | tf_op jit(solution)/shard_map/nrc,nrs->ncs/dot_general | solution.py:183
  10.9 0.0 copy-done.2
  10.9 1.8 fusion.21
  12.7 1.9 fusion.17
  14.6 1.8 fusion.13
  16.4 1.4 fusion.9
  17.8 0.0 copy-done.9
  17.8 0.3 fusion.45
  18.1 3.4 %broadcast_in_dim.2 = f32[24,256,256]{2,1,0:T(8,128)} broadcast(f32[]{:T(128)} %constant.22.clone.1), dimensions={} | broadcast | bytes 6291460 | tf_op jit(solution)/shard_map/broadcast_in_dim | solution.py:181
  21.5 5.1 %scatter_fusion = f32[24,256,256]{2,1,0:T(8,128)} fusion(f32[24,256,256]{2,1,0:T(8,128)} %broadcast_in_dim.2, s32[8]{0:T(128)S(1)} %get-tuple-element.6, f32[8,256,256]{2,1,0:T(8,128)} %fusion.25), kind=kCustom, calls=%fused_computation.5 | custom fusion | flops 524288 | bytes 6291488 | tf_op jit(solution)/shard_map/scatter-add | solution.py:186
  26.6 4.9 %scatter_fusion.1 = f32[24,256,256]{2,1,0:T(8,128)} fusion(f32[24,256,256]{2,1,0:T(8,128)} %scatter_fusion, s32[8]{0:T(128)S(1)} %get-tuple-element.5, f32[8,256,256]{2,1,0:T(8,128)} %fusion.21), kind=kCustom, calls=%fused_computation.6 | custom fusion | flops 524288 | bytes 6291488 | tf_op jit(solution)/shard_map/scatter-add | solution.py:186
  31.5 5.1 %scatter_fusion.2 = f32[24,256,256]{2,1,0:T(8,128)} fusion(f32[24,256,256]{2,1,0:T(8,128)} %scatter_fusion.1, s32[8]{0:T(128)S(1)} %get-tuple-element.4, f32[8,256,256]{2,1,0:T(8,128)} %fusion.17), kind=kCustom, calls=%fused_computation.7 | custom fusion | flops 524288 | bytes 6291488 | tf_op jit(solution)/shard_map/scatter-add | solution.py:186
  36.6 5.0 %scatter_fusion.3 = f32[24,256,256]{2,1,0:T(8,128)} fusion(f32[24,256,256]{2,1,0:T(8,128)} %scatter_fusion.2, s32[8]{0:T(128)S(1)} %get-tuple-element.3, f32[8,256,256]{2,1,0:T(8,128)} %fusion.13), kind=kCustom, calls=%fused_computation.8 | custom fusion | flops 524288 | bytes 6291488 | tf_op jit(solution)/shard_map/scatter-add | solution.py:186
  41.5 4.4 %scatter_fusion.4 = f32[24,256,256]{2,1,0:T(8,128)} fusion(f32[24,256,256]{2,1,0:T(8,128)} %scatter_fusion.3, s32[8]{0:T(128)S(1)} %get-tuple-element.2, f32[8,256,256]{2,1,0:T(8,128)S(1)} %fusion.9), kind=kCustom, calls=%fused_computation.9 | custom fusion | flops 524288 | bytes 6291488 | tf_op jit(solution)/shard_map/scatter-add | solution.py:186
  45.9 4.6 %fusion.47 = (f32[8,256,256]{2,1,0:T(8,128)}, f32[8,256,256]{2,1,0:T(8,128)}) fusion(f32[24,256,256]{2,1,0:T(8,128)} %scatter_fusion.4), kind=kLoop, calls=%fused_computation.85 | loop fusion | bytes 8388608 | tf_op jit(solution)/shard_map/slice | solution.py:187
  50.6 5.0 %collective-permute-start.3 = (f32[8,256,256]{2,1,0:T(8,128)}, f32[8,256,256]{2,1,0:T(8,128)S(1)}, u32[]{:S(2)}, u32[]{:S(2)}) collective-permute-start(f32[8,256,256]{2,1,0:T(8,128)} %get-tuple-element.16), channel_id=1, source_target_pairs={{0,4},{4,8},{8,12},{12,16},{16,20},{20,24},{24,28},{28,32},{32,36}... | collective-permute-start | bytes 6291464 | tf_op jit(solution)/shard_map/ppermute | solution.py:29
  55.6 5.2 %collective-permute-start.2 = (f32[8,256,256]{2,1,0:T(8,128)}, f32[8,256,256]{2,1,0:T(8,128)}, u32[]{:S(2)}, u32[]{:S(2)}) collective-permute-start(f32[8,256,256]{2,1,0:T(8,128)} %get-tuple-element.15), channel_id=1, source_target_pairs={{4,0},{8,4},{12,8},{16,12},{20,16},{24,20},{28,24},{32,28},{36,32}... | collective-permute-start | bytes 6291464 | tf_op jit(solution)/shard_map/ppermute | solution.py:29
  60.8 0.0 all-gather.2.cloned.1.call-update
  60.8 0.0 reduce-scatter.2.cloned.1.call-start
  60.9 18.0 %collective-permute-done.3 = f32[8,256,256]{2,1,0:T(8,128)S(1)} collective-permute-done((f32[8,256,256]{2,1,0:T(8,128)}, f32[8,256,256]{2,1,0:T(8,128)S(1)}, u32[]{:S(2)}, u32[]{:S(2)}) %collective-permute-start.3) | collective-permute-done | bytes 2097184 | tf_op jit(solution)/shard_map/ppermute | solution.py:29
  78.8 4.4 %collective-permute-done.2 = f32[8,256,256]{2,1,0:T(8,128)} collective-permute-done((f32[8,256,256]{2,1,0:T(8,128)}, f32[8,256,256]{2,1,0:T(8,128)}, u32[]{:S(2)}, u32[]{:S(2)}) %collective-permute-start.2) | collective-permute-done | bytes 2097184 | tf_op jit(solution)/shard_map/ppermute | solution.py:29
  83.2 4.0 %fusion = f32[8,256,256]{2,1,0:T(8,128)} fusion(f32[8,256,256]{2,1,0:T(8,128)S(1)} %collective-permute-done.3, f32[8,256,256]{2,1,0:T(8,128)} %collective-permute-done.2, f32[24,256,256]{2,1,0:T(8,128)} %scatter_fusion.4), kind=kLoop, calls=%fused_computation.11 | loop fusion | flops 1048576 | bytes 8388608 | tf_op jit(solution)/shard_map/add | solution.py:189
  87.2 0.0 reduce-scatter.2.cloned.1.call-update
  87.2 6.6 %all-gather.2.cloned.1.call-done = bf16[8,256,256]{2,1,0:T(8,128)(2,1)} async-done(((bf16[8,64,256]{2,1,0:T(8,128)(2,1)}), bf16[8,256,256]{2,1,0:T(8,128)(2,1)}) %all-gather.2.cloned.1.call-update) | async-done | bytes 1048592 | tf_op jit(solution)/shard_map/all_gather | solution.py:172
  93.8 4.8 %collective-permute-start = (bf16[8,256,256]{2,1,0:T(8,128)(2,1)}, bf16[8,256,256]{2,1,0:T(8,128)(2,1)S(1)}, u32[]{:S(2)}, u32[]{:S(2)}) collective-permute-start(bf16[8,256,256]{2,1,0:T(8,128)(2,1)} %all-gather.2.cloned.1.call-done), channel_id=1, source_target_pairs={{0,4},{4,8},{8,12},{12,16},{16,20},{20,24},{24,28},{28,32},{32,36}... | collective-permute-start | bytes 3145736 | tf_op jit(solution)/shard_map/ppermute | solution.py:20
  98.6 1.9 collective-permute-start.1
  100.6 10.1 %collective-permute-done = bf16[8,256,256]{2,1,0:T(8,128)(2,1)S(1)} collective-permute-done((bf16[8,256,256]{2,1,0:T(8,128)(2,1)}, bf16[8,256,256]{2,1,0:T(8,128)(2,1)S(1)}, u32[]{:S(2)}, u32[]{:S(2)}) %collective-permute-start) | collective-permute-done | bytes 1048608 | tf_op jit(solution)/shard_map/ppermute | solution.py:20
  110.7 0.1 constant_dynamic-update-slice_fusion.2
  110.7 0.0 copy-done.7
  110.7 0.1 constant_dynamic-update-slice_fusion.1
  110.8 4.1 %collective-permute-done.1 = bf16[8,256,256]{2,1,0:T(8,128)(2,1)S(1)} collective-permute-done((bf16[8,256,256]{2,1,0:T(8,128)(2,1)}, bf16[8,256,256]{2,1,0:T(8,128)(2,1)S(1)}, u32[]{:S(2)}, u32[]{:S(2)}) %collective-permute-start.1) | collective-permute-done | bytes 1048608 | tf_op jit(solution)/shard_map/ppermute | solution.py:21
  115.0 0.1 constant_dynamic-update-slice_fusion
  115.0 1.6 gather_fusion.4
  116.6 1.6 gather_fusion.3
  118.3 1.6 gather_fusion.2
  119.9 1.6 gather_fusion.1
  121.5 1.6 gather_fusion
  123.1 1.8 fusion.11
  124.8 1.7 fusion.15
  126.6 0.3 fusion.19
  126.9 0.3 fusion.23
  127.2 0.6 copy-done.6
  127.8 0.3 fusion.4
  128.1 12.0 %all_to_all.15 = f32[8,64,256]{2,1,0:T(8,128)S(1)} all-to-all(f32[8,64,256]{2,1,0:T(8,128)S(1)} %fusion.4), channel_id=1, replica_groups=mesh['row'=128,'col'=4] {'col'}, dimensions={0} | all-to-all | bytes 1048576 | tf_op jit(solution)/shard_map/all_to_all | solution.py:180
  140.2 0.0 reduce-scatter.2.cloned.1.call-done
  140.2 2.0 %fusion.5.wide = f32[2,2,256,128]{3,2,1,0:T(8,128)S(1)} fusion(f32[1,2,256,256]{3,2,1,0:T(8,128)} %bitcast.112, f32[1,2,256,256]{3,2,1,0:T(8,128)S(1)} %bitcast.110, f32[256,128]{1,0:T(8,128)S(1)} %copy-done.8), kind=kOutput, calls=%fused_computation.17 | convolution fusion | flops 402915328 | bytes 1703936 | tf_op jit(solution)/shard_map/...bs,sk->...bk/dot_general | solution.py:193
  142.3 1.1 fusion.48.gram
  143.3 2.2 %collective-permute-start.4 = (f32[2,128,128]{2,1,0:T(8,128)S(1)}, f32[2,128,128]{2,1,0:T(8,128)S(1)}, u32[]{:S(2)}, u32[]{:S(2)}) collective-permute-start(f32[2,128,128]{2,1,0:T(8,128)S(1)} %fusion.39.own1), channel_id=1, source_target_pairs={{0,1},{1,0},{2,3},{3,2},{4,5},{5,4},{6,7},{7,6},{8,9},{9,8},{10,11... | collective-permute-start | bytes 393224 | tf_op jit(solution)/shard_map/ppermute | solution.py:33
  145.6 0.1 stack.68.bits
  145.7 4.2 %collective-permute-done.4 = f32[2,128,128]{2,1,0:T(8,128)S(1)} collective-permute-done((f32[2,128,128]{2,1,0:T(8,128)S(1)}, f32[2,128,128]{2,1,0:T(8,128)S(1)}, u32[]{:S(2)}, u32[]{:S(2)}) %collective-permute-start.4) | collective-permute-done | bytes 131104 | tf_op jit(solution)/shard_map/ppermute | solution.py:33
  149.9 2.7 %collective-permute-start.5 = (f32[2,128,128]{2,1,0:T(8,128)S(1)}, f32[2,128,128]{2,1,0:T(8,128)S(1)}, u32[]{:S(2)}, u32[]{:S(2)}) collective-permute-start(f32[2,128,128]{2,1,0:T(8,128)S(1)} %get-tuple-element.14), channel_id=1, source_target_pairs={{0,2},{1,3},{2,0},{3,1},{4,6},{5,7},{6,4},{7,5},{8,10},{9,11},{10,... | collective-permute-start | bytes 393224 | tf_op jit(solution)/shard_map/ppermute | solution.py:33
  152.6 4.5 %collective-permute-done.5 = f32[2,128,128]{2,1,0:T(8,128)S(1)} collective-permute-done((f32[2,128,128]{2,1,0:T(8,128)S(1)}, f32[2,128,128]{2,1,0:T(8,128)S(1)}, u32[]{:S(2)}, u32[]{:S(2)}) %collective-permute-start.5) | collective-permute-done | bytes 131104 | tf_op jit(solution)/shard_map/ppermute | solution.py:33
  157.1 4.4 %collective-permute-start.6 = (f32[2,128,128]{2,1,0:T(8,128)S(1)}, f32[2,128,128]{2,1,0:T(8,128)S(1)}, u32[]{:S(2)}, u32[]{:S(2)}) collective-permute-start(f32[2,128,128]{2,1,0:T(8,128)S(1)} %get-tuple-element.12), channel_id=1, source_target_pairs={{0,4},{4,0},{8,12},{12,8},{16,20},{20,16},{24,28},{28,24},{32,36},... | collective-permute-start | bytes 393224 | tf_op jit(solution)/shard_map/ppermute | solution.py:33
  161.5 0.9 collective-permute-done.6
  162.5 3.3 %collective-permute-start.7 = (f32[2,128,128]{2,1,0:T(8,128)S(1)}, f32[2,128,128]{2,1,0:T(8,128)S(1)}, u32[]{:S(2)}, u32[]{:S(2)}) collective-permute-start(f32[2,128,128]{2,1,0:T(8,128)S(1)} %get-tuple-element.10), channel_id=1, source_target_pairs={{0,8},{4,12},{8,0},{12,4},{16,24},{20,28},{24,16},{28,20},{32,40},... | collective-permute-start | bytes 393224 | tf_op jit(solution)/shard_map/ppermute | solution.py:33
  165.8 3.3 %collective-permute-done.7 = f32[2,128,128]{2,1,0:T(8,128)S(1)} collective-permute-done((f32[2,128,128]{2,1,0:T(8,128)S(1)}, f32[2,128,128]{2,1,0:T(8,128)S(1)}, u32[]{:S(2)}, u32[]{:S(2)}) %collective-permute-start.7) | collective-permute-done | bytes 131104 | tf_op jit(solution)/shard_map/ppermute | solution.py:33
  169.1 4.2 %collective-permute-start.8 = (f32[2,128,128]{2,1,0:T(8,128)S(1)}, f32[2,128,128]{2,1,0:T(8,128)S(1)}, u32[]{:S(2)}, u32[]{:S(2)}) collective-permute-start(f32[2,128,128]{2,1,0:T(8,128)S(1)} %get-tuple-element.8), channel_id=1, source_target_pairs={{0,16},{4,20},{8,24},{12,28},{16,0},{20,4},{24,8},{28,12},{32,48},... | collective-permute-start | bytes 393224 | tf_op jit(solution)/shard_map/ppermute | solution.py:33
  173.4 5.6 %collective-permute-done.8 = f32[2,128,128]{2,1,0:T(8,128)S(1)} collective-permute-done((f32[2,128,128]{2,1,0:T(8,128)S(1)}, f32[2,128,128]{2,1,0:T(8,128)S(1)}, u32[]{:S(2)}, u32[]{:S(2)}) %collective-permute-start.8) | collective-permute-done | bytes 131104 | tf_op jit(solution)/shard_map/ppermute | solution.py:33
  179.1 0.0 copy-done.1
  179.1 13.5 %shard_map.77 = (bf16[2,2,256,128]{3,2,1,0:T(8,128)(2,1)}, bf16[2,1,5,256,128]{4,3,2,1,0:T(8,128)(2,1)}) custom-call(s32[5]{0:T(128)S(1)} %stack.68.bits, s32[6]{0:T(128)S(1)} %copy-done.1, f32[2,2,256,128]{3,2,1,0:T(8,128)S(1)} %fusion.5.wide, f32[2,2,128,128]{3,2,1,0:T(8,128)S(1)} %fusion.48.gram, f32[2,128,128]{2,1,0:T(8,128)S(1)} %fusion.39.own1, ...), custom_call_target="tpu_custom_call" | custom-call | tf_op jit(solution)/shard_map/pallas_call | solution.py:153
  (29 shorter events, 0.3 us)
Async XLA Ops:
  7.2 1.0 copy-start
  7.2 3.7 %copy-start.2 = (bf16[8,5,64,256]{3,2,1,0:T(8,128)(2,1)S(1)}, bf16[8,5,64,256]{3,2,1,0:T(8,128)(2,1)}, u32[]{:S(2)}) copy-start(bf16[8,5,64,256]{3,2,1,0:T(8,128)(2,1)} %param.6) | copy-start | bytes 3932164
  7.2 86.7 %all-gather.2.cloned.1.call-start = ((), (), s32[]{:S(2)}) async-start(), calls=%async_computation.2 | async-start | bytes 1310720 | tf_op jit(solution)/shard_map/all_gather | solution.py:172
  14.6 3.3 %copy-start.9 = (s32[8,5]{1,0:T(8,128)S(1)}, s32[8,5]{1,0:T(8,128)}, u32[]{:S(2)}) copy-start(s32[8,5]{1,0:T(8,128)} %param.10) | copy-start | bytes 484
  50.6 28.3 %collective-permute-start.3 = (f32[8,256,256]{2,1,0:T(8,128)}, f32[8,256,256]{2,1,0:T(8,128)S(1)}, u32[]{:S(2)}, u32[]{:S(2)}) collective-permute-start(f32[8,256,256]{2,1,0:T(8,128)} %get-tuple-element.16), channel_id=1, source_target_pairs={{0,4},{4,8},{8,12},{12,16},{16,20},{20,24},{24,28},{28,32},{32,36}... | collective-permute-start | bytes 6291464 | tf_op jit(solution)/shard_map/ppermute | solution.py:29
  55.6 27.7 %collective-permute-start.2 = (f32[8,256,256]{2,1,0:T(8,128)}, f32[8,256,256]{2,1,0:T(8,128)}, u32[]{:S(2)}, u32[]{:S(2)}) collective-permute-start(f32[8,256,256]{2,1,0:T(8,128)} %get-tuple-element.15), channel_id=1, source_target_pairs={{4,0},{8,4},{12,8},{16,12},{20,16},{24,20},{28,24},{32,28},{36,32}... | collective-permute-start | bytes 6291464 | tf_op jit(solution)/shard_map/ppermute | solution.py:29
  60.8 79.4 %reduce-scatter.2.cloned.1.call-start = ((), (), s32[]{:S(2)}) async-start(), calls=%async_computation.3 | async-start | bytes 2621440 | tf_op jit(solution)/shard_map/reduce_scatter | solution.py:190
  93.8 16.9 %copy-start.7 = (bf16[8,256,256]{2,1,0:T(8,128)(2,1)S(1)}, bf16[8,256,256]{2,1,0:T(8,128)(2,1)}, u32[]{:S(2)}) copy-start(bf16[8,256,256]{2,1,0:T(8,128)(2,1)} %all-gather.2.cloned.1.call-done) | copy-start | bytes 3145732
  93.8 16.8 %collective-permute-start = (bf16[8,256,256]{2,1,0:T(8,128)(2,1)}, bf16[8,256,256]{2,1,0:T(8,128)(2,1)S(1)}, u32[]{:S(2)}, u32[]{:S(2)}) collective-permute-start(bf16[8,256,256]{2,1,0:T(8,128)(2,1)} %all-gather.2.cloned.1.call-done), channel_id=1, source_target_pairs={{0,4},{4,8},{8,12},{12,16},{16,20},{20,24},{24,28},{28,32},{32,36}... | collective-permute-start | bytes 3145736 | tf_op jit(solution)/shard_map/ppermute | solution.py:20
  98.6 16.3 %collective-permute-start.1 = (bf16[8,256,256]{2,1,0:T(8,128)(2,1)}, bf16[8,256,256]{2,1,0:T(8,128)(2,1)S(1)}, u32[]{:S(2)}, u32[]{:S(2)}) collective-permute-start(bf16[8,256,256]{2,1,0:T(8,128)(2,1)} %all-gather.2.cloned.1.call-done), channel_id=1, source_target_pairs={{4,0},{8,4},{12,8},{16,12},{20,16},{24,20},{28,24},{32,28},{36,32}... | collective-permute-start | bytes 3145736 | tf_op jit(solution)/shard_map/ppermute | solution.py:21
  123.1 3.5 %copy-start.3 = (bf16[8,5,64,256]{3,2,1,0:T(8,128)(2,1)S(1)}, bf16[8,5,64,256]{3,2,1,0:T(8,128)(2,1)}, u32[]{:S(2)}) copy-start(bf16[8,5,64,256]{3,2,1,0:T(8,128)(2,1)} %param.6) | copy-start | bytes 3932164
  123.1 3.5 %copy-start.4 = (bf16[8,256,256]{2,1,0:T(8,128)(2,1)S(1)}, bf16[8,256,256]{2,1,0:T(8,128)(2,1)}, u32[]{:S(2)}) copy-start(bf16[8,256,256]{2,1,0:T(8,128)(2,1)} %gather_fusion.2) | copy-start | bytes 3145732
  124.8 2.1 %copy-start.5 = (bf16[8,256,256]{2,1,0:T(8,128)(2,1)S(1)}, bf16[8,256,256]{2,1,0:T(8,128)(2,1)}, u32[]{:S(2)}) copy-start(bf16[8,256,256]{2,1,0:T(8,128)(2,1)} %gather_fusion.1) | copy-start | bytes 3145732
  126.6 1.2 copy-start.6
  127.8 12.4 %copy-start.8 = (f32[256,128]{1,0:T(8,128)S(1)}, f32[256,128]{1,0:T(8,128)}, u32[]{:S(2)}) copy-start(f32[256,128]{1,0:T(8,128)} %param.9) | copy-start | bytes 393220
  143.3 6.5 %collective-permute-start.4 = (f32[2,128,128]{2,1,0:T(8,128)S(1)}, f32[2,128,128]{2,1,0:T(8,128)S(1)}, u32[]{:S(2)}, u32[]{:S(2)}) collective-permute-start(f32[2,128,128]{2,1,0:T(8,128)S(1)} %fusion.39.own1), channel_id=1, source_target_pairs={{0,1},{1,0},{2,3},{3,2},{4,5},{5,4},{6,7},{7,6},{8,9},{9,8},{10,11... | collective-permute-start | bytes 393224 | tf_op jit(solution)/shard_map/ppermute | solution.py:33
  149.9 7.2 %collective-permute-start.5 = (f32[2,128,128]{2,1,0:T(8,128)S(1)}, f32[2,128,128]{2,1,0:T(8,128)S(1)}, u32[]{:S(2)}, u32[]{:S(2)}) collective-permute-start(f32[2,128,128]{2,1,0:T(8,128)S(1)} %get-tuple-element.14), channel_id=1, source_target_pairs={{0,2},{1,3},{2,0},{3,1},{4,6},{5,7},{6,4},{7,5},{8,10},{9,11},{10,... | collective-permute-start | bytes 393224 | tf_op jit(solution)/shard_map/ppermute | solution.py:33
  157.1 22.0 %copy-start.1 = (s32[6]{0:T(128)S(1)}, s32[6]{0:T(128)}, u32[]{:S(2)}) copy-start(s32[6]{0:T(128)} %ranks.1) | copy-start | bytes 76
  157.1 5.3 %collective-permute-start.6 = (f32[2,128,128]{2,1,0:T(8,128)S(1)}, f32[2,128,128]{2,1,0:T(8,128)S(1)}, u32[]{:S(2)}, u32[]{:S(2)}) collective-permute-start(f32[2,128,128]{2,1,0:T(8,128)S(1)} %get-tuple-element.12), channel_id=1, source_target_pairs={{0,4},{4,0},{8,12},{12,8},{16,20},{20,16},{24,28},{28,24},{32,36},... | collective-permute-start | bytes 393224 | tf_op jit(solution)/shard_map/ppermute | solution.py:33
  162.5 6.6 %collective-permute-start.7 = (f32[2,128,128]{2,1,0:T(8,128)S(1)}, f32[2,128,128]{2,1,0:T(8,128)S(1)}, u32[]{:S(2)}, u32[]{:S(2)}) collective-permute-start(f32[2,128,128]{2,1,0:T(8,128)S(1)} %get-tuple-element.10), channel_id=1, source_target_pairs={{0,8},{4,12},{8,0},{12,4},{16,24},{20,28},{24,16},{28,20},{32,40},... | collective-permute-start | bytes 393224 | tf_op jit(solution)/shard_map/ppermute | solution.py:33
  169.1 9.9 %collective-permute-start.8 = (f32[2,128,128]{2,1,0:T(8,128)S(1)}, f32[2,128,128]{2,1,0:T(8,128)S(1)}, u32[]{:S(2)}, u32[]{:S(2)}) collective-permute-start(f32[2,128,128]{2,1,0:T(8,128)S(1)} %get-tuple-element.8), channel_id=1, source_target_pairs={{0,16},{4,20},{8,24},{12,28},{16,0},{20,4},{24,8},{28,12},{32,48},... | collective-permute-start | bytes 393224 | tf_op jit(solution)/shard_map/ppermute | solution.py:33
Sparse Core Ops, SparseCore 0:
  60.9 32.8 all-gather.1
  96.7 42.7 reduce-scatter.1

commit v2 on v1

--- a/solution.py
+++ b/solution.py
@@ -6,32 +6,6 @@
 from jax.experimental import pallas as pl
 from jax.experimental.pallas import tpu as pltpu
 from jax.sharding import PartitionSpec as P
-
-ROW_LEVELS = 3
-
-
-def padded(value, sides, width):
-    for axis, dim in sides:
-        size, length = (lax.axis_size(axis), value.shape[dim])
-        up = [(i, (i + 1) % size) for i in range(size - 1)]
-        down = [(j, i) for i, j in up]
-        last = lax.slice_in_dim(value, length - width, length, axis=dim)
-        initial = lax.slice_in_dim(value, 0, width, axis=dim)
-        before = lax.ppermute(last, axis, up)
-        after = lax.ppermute(initial, axis, down)
-        value = jnp.concatenate([before, value, after], axis=dim)
-    return value
-
-
-def passed_along(value, axis, by):
-    size = lax.axis_size(axis)
-    pairs = [(i, i + by) for i in range(size) if 0 <= i + by < size]
-    return lax.ppermute(value, axis, pairs)
-
-
-def partner(value, axis, distance):
-    return lax.ppermute(value, axis, [(i, i ^ 1 << distance) for i in range(lax.axis_size(axis))])
-
 
 K = 128
 F32 = jnp.float32
@@ -104,7 +78,7 @@
     b = cat([v.astype(BF16) for v in pieces(y)], "hmhlmh")
     return lax.dot_general(a, b, (((1,), (1,)), ((), ())), preferred_element_type=F32)
 
-def kernel(bits, ranks, wide, gram, own1, chain, sib, leaf_out, tr_out, S, E):
+def kernel(bits, ranks, wide, gram, chain, sib, leaf_out, tr_out, S, E):
     eye = (lax.broadcasted_iota(jnp.int32, (K, K), 0) == lax.broadcasted_iota(jnp.int32, (K, K), 1)).astype(F32)
     def place(i, x):
         put(S, i // 8, i % 8, x)
@@ -112,9 +86,9 @@
         for l in range(2):
             place(s * 2 + l, gram[s, l])
         for j in range(5):
-            place(4 + s * 5 + j, chain[s, j])
-            place(18 + s * 5 + j, sib[s, j])
-        place(16 + s, own1[s])
+            place(4 + s * 5 + j, chain[j + 1, s])
+            place(18 + s * 5 + j, sib[j, s])
+        place(16 + s, chain[0, s])
     for i in (14, 15, 28, 29, 30, 31):
         place(i, eye)
     for g in range(2):
@@ -147,65 +121,224 @@
             tr_out[s, 0, j, pl.ds(pl.multiple_of(up * K, K), K), :] = (exact_nt(own, x) * keep).astype(BF16)
             tr_out[s, 0, j, pl.ds(pl.multiple_of((1 - up) * K, K), K), :] = (exact_nt(other, x) * keep).astype(BF16)
 
-def finish(bits, ranks, wide, gram, own1, chain, sib):
+def finish(bits, ranks, wide, gram, chain, sib):
     vm = pl.BlockSpec(memory_space=pltpu.VMEM)
     sm = pl.BlockSpec(memory_space=pltpu.SMEM)
     return pl.pallas_call(
         kernel,
         out_shape=(jax.ShapeDtypeStruct((2, 2, 256, K), BF16), jax.ShapeDtypeStruct((2, 1, 5, 256, K), BF16)),
-        in_specs=[sm, sm, vm, vm, vm, vm, vm],
+        in_specs=[sm, sm, vm, vm, vm, vm],
         out_specs=(vm, vm),
         scratch_shapes=[pltpu.VMEM((4 * 1024, K), F32), pltpu.VMEM((2 * 1024, K), F32)],
         compiler_params=pltpu.CompilerParams(vmem_limit_bytes=48 << 20),
-    )(bits, ranks, wide, gram, own1, chain, sib)
+    )(bits, ranks, wide, gram, chain, sib)
+
+
+def dot(a, b):
+    return jnp.dot(a, b, preferred_element_type=F32)
+
+
+def dot_nt(a, b):
+    return lax.dot_general(a, b, (((1,), (1,)), ((), ())), preferred_element_type=F32)
+
+
+def halves(x):
+    return [v.astype(BF16) for v in pieces(x)]
+
+
+def remote(src, dst, send, recv, row, col):
+    return pltpu.make_async_remote_copy(
+        src_ref=src, dst_ref=dst, send_sem=send, recv_sem=recv,
+        device_id=(row, col), device_id_type=pl.DeviceIdType.MESH,
+    )
+
+
+def sketch_kernel(
+    lidx, blocks, samples, probes, compress,
+    wide_out, gram_out, chain_out, sib_out,
+    S, T1, T3, TO, TI, VP, RO, RI, WO, WI, CH, SB,
+    own_sem, xs_send, xs_recv, zs_send, zs_recv, t_send, t_recv, r_send, r_recv, w_send, w_recv, b_send, b_recv,
+):
+    row, col = lax.axis_index("row"), lax.axis_index("col")
+    rows, cols = lax.axis_size("row"), lax.axis_size("col")
+    around = [(row + rows - 1) % rows, (row + 1) % rows]
+    peer = [(col + s) % cols for s in range(4)]
+    source = [(col + cols - s) % cols for s in range(4)]
+    bit = lambda x, n: x // (1 << n) % 2
+    flip = lambda x, n: x + (1 << n) * (1 - 2 * bit(x, n))
+    mates = [(row, flip(col, 0)), (row, flip(col, 1))] + [(flip(row, n), col) for n in range(3)]
+
+    barrier = pltpu.get_barrier_semaphore()
+    greet = [(row, peer[s]) for s in (1, 2, 3)] + [(r, col) for r in around] + mates[3:]
+    for device in greet:
+        pl.semaphore_signal(barrier, inc=1, device_id=device, device_id_type=pl.DeviceIdType.MESH)
+    pl.semaphore_wait(barrier, len(greet))
+
+    part = lambda c: pl.ds(pl.multiple_of(64 * c, 64), 64)
+    pair = lambda q: pl.ds(2 * q, 2)
+    gather = {}
+    for s in (2, 1, 3):
+        gather[s] = remote(samples, S.at[pl.ds(8, 8), part(col)], xs_send.at[s], xs_recv.at[s], row, peer[s])
+        gather[s].start()
+    spread = {}
+    for d in (0, 1):
+        spread[d, 0] = remote(samples, S.at[pl.ds(16 - 16 * d, 8), part(col)], zs_send.at[d, 0], zs_recv.at[d, 0], around[d], col)
+        spread[d, 0].start()
+    own = pltpu.make_async_copy(samples, S.at[pl.ds(8, 8), part(col)], own_sem)
+    own.start()
+
+    ch, cm, cl = halves(compress[...])
+    ct = jnp.concatenate(halves(compress[...].T), axis=1)
+    left = []
+    for i in range(8):
+        p = probes[i]
+        zt = dot_nt(ct, jnp.concatenate([p, p, p], axis=1))
+        left.append(jnp.concatenate(halves(zt), axis=1))
+    def term(i, k):
+        b = blocks[i, k]
+        return dot(left[i], jnp.concatenate([b, b, b], axis=0))
+    for i in range(8):
+        T1[i] = term(i, 1)
+        T3[i] = term(i, 3)
+    on = lambda i, k, j: jnp.where(lidx[i, k] == j, 1.0, 0.0).astype(F32)
+    for j in range(8):
+        up = term(j, 0)
+        for i in range(j):
+            up = up + on(i, 1, j) * T1[i]
+        TO[0, j] = up
+        down = term(j, 4)
+        for i in range(j + 1, 8):
+            down = down + on(i, 3, 16 + j) * T3[i]
+        TO[1, j] = down
+    order = (2, 1, 3, 0)
+    terms = {}
+    for s in order:
+        for d in (0, 1):
+            terms[d, s] = remote(TO.at[d, pair(peer[s])], TI.at[1 - d, pair(peer[s])], t_send.at[d, s], t_recv.at[1 - d, s], around[d], col)
+            terms[d, s].start()
+    for j in range(8):
+        mid = term(j, 2)
+        for i in range(j + 1, 8):
+            mid = mid + on(i, 1, 8 + j) * T1[i]
+        for i in range(j):
+            mid = mid + on(i, 3, 8 + j) * T3[i]
+        VP[j] = mid
+
+    for s in (1, 3, 2):
+        gather[s].wait_recv()
+        for d in (0, 1):
+            here = S.at[pl.ds(8, 8), part(source[s])]
+            there = S.at[pl.ds(16 - 16 * d, 8), part(source[s])]
+            spread[d, s] = remote(here, there, zs_send.at[d, s], zs_recv.at[d, s], around[d], col)
+            spread[d, s].start()
+
+    has = [jnp.where(row > 0, 1.0, 0.0).astype(F32), jnp.where(row < rows - 1, 1.0, 0.0).astype(F32)]
+    reduce = {}
+    for s in order:
+        for d in (0, 1):
+            remote(TO.at[d, pair(peer[s])], TI.at[d, pair(peer[s])], t_send.at[d, s], t_recv.at[d, s], around[d], col).wait_recv()
+        total = VP[pair(peer[s])] + has[0] * TI[0, pair(peer[s])] + has[1] * TI[1, pair(peer[s])]
+        RO[s] = total
+        if s:
+            reduce[s] = remote(RO.at[s], RI.at[s], r_send.at[s], r_recv.at[s], row, peer[s])
+            reduce[s].start()
+
+    own.wait()
+    for s in (0, 1, 3, 2):
+        for d in (0, 1):
+            remote(samples, S.at[pl.ds(16 * d, 8), part(source[s])], zs_send.at[d, s], zs_recv.at[1 - d, s], around[d], col).wait_recv()
+    cc = jnp.concatenate([ch, cm, cl, ch, cm, ch], axis=0)
+    share = {}
+    for s in order:
+        acc = []
+        for e in range(2):
+            n = 2 * peer[s] + e
+            total = dot(blocks[n, 2], S[8 + n])
+            total = total + has[0] * dot(blocks[n, 0], S[n])
+            total = total + has[1] * dot(blocks[n, 4], S[16 + n])
+            for k, d in ((1, 0), (3, 1)):
+                where = lidx[n, k]
+                outside = jnp.where(where < 8, has[0], jnp.where(where >= 16, has[1], 1.0))
+                total = total + outside * dot(blocks[n, k], S[where])
+            acc.append(total)
+        h, m, l = halves(jnp.concatenate(acc, axis=0))
+        w = dot(jnp.concatenate([h, h, h, m, m, l], axis=1), cc)
+        WO[s] = w.reshape(2, 64, K)
+        if s:
+            share[s] = remote(WO.at[s], WI.at[:, part(col)], w_send.at[s], w_recv.at[s], row, peer[s])
+            share[s].start()
+        else:
+            WI[:, part(col)] = w.reshape(2, 64, K)
+
+    for s in (1, 3, 2):
+        reduce[s].wait_recv()
+    for l in range(2):
+        vt = RO[0, l] + RI[1, l] + RI[3, l] + RI[2, l]
+        wide_out[1, l] = vt.T
+        gram_out[1, l] = exact_nt(vt, vt)
+    for s in (1, 3, 2):
+        share[s].wait_recv()
+    for l in range(2):
+        wt = WI[l].T
+        wide_out[0, l] = WI[l]
+        gram_out[0, l] = exact_nt(wt, wt)
+    for side in range(2):
+        CH[0, side] = gram_out[side, 0] + gram_out[side, 1]
+    swaps = []
+    for j in range(5):
+        swaps.append(remote(CH.at[j], SB.at[j], b_send.at[j], b_recv.at[j], *mates[j]))
+        swaps[j].start()
+        swaps[j].wait_recv()
+        CH[j + 1] = CH[j] + SB[j]
+    for j in range(6):
+        chain_out[j] = CH[j]
+    for j in range(5):
+        sib_out[j] = SB[j]
+    for copies in (gather, spread, terms, reduce, share):
+        for c in copies.values():
+            c.wait_send()
+    for c in swaps:
+        c.wait_send()
+
+
+def sketch(lidx, blocks, samples, probes, compress):
+    vm = pl.BlockSpec(memory_space=pltpu.VMEM)
+    sm = pl.BlockSpec(memory_space=pltpu.SMEM)
+    dma = pltpu.SemaphoreType.DMA
+    shape = jax.ShapeDtypeStruct
+    return pl.pallas_call(
+        sketch_kernel,
+        out_shape=(
+            shape((2, 2, 256, K), F32), shape((2, 2, K, K), F32),
+            shape((6, 2, K, K), F32), shape((5, 2, K, K), F32),
+        ),
+        in_specs=[sm, vm, vm, vm, vm],
+        out_specs=(vm, vm, vm, vm),
+        scratch_shapes=[
+            pltpu.VMEM((24, 256, 256), BF16),
+            pltpu.VMEM((8, K, 256), F32), pltpu.VMEM((8, K, 256), F32),
+            pltpu.VMEM((2, 8, K, 256), F32), pltpu.VMEM((2, 8, K, 256), F32),
+            pltpu.VMEM((8, K, 256), F32),
+            pltpu.VMEM((4, 2, K, 256), F32), pltpu.VMEM((4, 2, K, 256), F32),
+            pltpu.VMEM((4, 2, 64, K), F32), pltpu.VMEM((2, 256, K), F32),
+            pltpu.VMEM((6, 2, K, K), F32), pltpu.VMEM((5, 2, K, K), F32),
+            dma, dma((4,)), dma((4,)), dma((2, 4)), dma((2, 4)), dma((2, 4)), dma((2, 4)),
+            dma((4,)), dma((4,)), dma((4,)), dma((4,)), dma((5,)), dma((5,)),
+        ],
+        compiler_params=pltpu.CompilerParams(
+            collective_id=0, has_side_effects=True, vmem_limit_bytes=48 << 20
+        ),
+    )(lidx, blocks, samples, probes, compress)
 
 
 def body(blocks, samples, probes, compress, pattern, ranks):
     row_index = lax.axis_index("row")
     col_index = lax.axis_index("col")
     n_blocks = blocks.shape[0]
-    n_slots = blocks.shape[1]
-    rows_block = blocks.shape[3]
-    n_samples = samples.shape[2]
-    rank_max = compress.shape[1]
     local_index = pattern - row_index * n_blocks + n_blocks
-    full_rows = lax.all_gather(samples, "col", axis=1, tiled=True)
-    extended = padded(full_rows, (("row", 0),), n_blocks)
-    partial_value = jnp.zeros((n_blocks, blocks.shape[2], n_samples), jnp.float32)
-    for slot in range(n_slots):
-        picked = extended[local_index[:, slot]]
-        partial_value = partial_value + jnp.einsum(
-            "nrc,ncs->nrs", blocks[:, slot], picked, preferred_element_type=jnp.float32
-        )
-    row_sketch = lax.all_to_all(partial_value, "col", split_axis=0, concat_axis=1, tiled=True)
-    buffer = jnp.zeros((3 * n_blocks, rows_block, n_samples), jnp.float32)
-    for slot in range(n_slots):
-        term = jnp.einsum(
-            "nrc,nrs->ncs", blocks[:, slot], probes, preferred_element_type=jnp.float32
-        )
-        buffer = buffer.at[local_index[:, slot]].add(term)
-    from_above = passed_along(buffer[:n_blocks], "row", -1)
-    from_below = passed_along(buffer[2 * n_blocks :], "row", 1)
-    adjoint_part = buffer[n_blocks : 2 * n_blocks] + from_above + from_below
-    col_sketch = lax.psum_scatter(adjoint_part, "col", scatter_dimension=0, tiled=True)
-    hp = lax.Precision.HIGHEST
-    sides = jnp.stack([row_sketch, col_sketch])
-    wide = jnp.einsum("...bs,sk->...bk", sides, compress, precision=hp)
-    gram = jnp.einsum("...bk,...bj->...kj", wide, wide, precision=hp)
-    current = gram[:, 0] + gram[:, 1]
-    chain = [current]
-    siblings = []
-    bits = []
-    for axis, index, levels in (("col", col_index, 2), ("row", row_index, ROW_LEVELS)):
-        for bit in range(levels):
-            other = partner(current, axis, bit)
-            current = current + other
-            siblings.append(other)
-            chain.append(current)
-            bits.append(index >> bit & 1)
-    return finish(
-        jnp.stack(bits), ranks, wide, gram, chain[0], jnp.stack(chain[1:], 1), jnp.stack(siblings, 1)
-    )
+    wide, gram, chain, sib = sketch(local_index, blocks, samples, probes, compress)
+    bits = jnp.stack([i >> n & 1 for i, n in ((col_index, 0), (col_index, 1), (row_index, 0), (row_index, 1), (row_index, 2))])
+    return finish(bits, ranks, wide, gram, chain, sib)
 
 
 def solution(mesh):

time: 200 us -> 84.6 us (0.42)
  the two profiles are of different devices: /device:TPU:1 before, /device:TPU:97 now
where the time goes in v2:
time: 84.6 us; the launch traced here: 84.4 us
  Pallas kernels  78.8 us (93%)
  local copies, waits for them, and re-layouts  4.21 us (5%)
    pallas_call x1, Pallas kernels, sketch(): pl.pallas_call(sketch_kernel, out_shape=(shape((2, 2, 256, K), F32), shap...  65.1 us
    pallas_call x1, Pallas kernels, finish(): pl.pallas_call(kernel, out_shape=(jax.ShapeDtypeStruct((2, 2, 256, K), BF...  13.7 us
    unnamed x10, local copies, waits for them, and re-layouts  4.12 us

profile of v2, /device:TPU:97, one launch (start us, length us, event | category | flops | bytes accessed | tf_op | source)
XLA Modules:
  0.0 84.4 jit_solution(17643792967225108243)
XLA Ops:
  0.6 0.0 copy-start.4
  0.6 0.1 stack.23.bits
  0.7 0.7 subtract_add_fusion.lidx
  1.4 0.0 copy-start
  1.4 1.3 %copy-done = bf16[8,5,64,256]{3,2,1,0:T(8,128)(2,1)S(1)} copy-done((bf16[8,5,64,256]{3,2,1,0:T(8,128)(2,1)S(1)}, bf16[8,5,64,256]{3,2,1,0:T(8,128)(2,1)}, u32[]{:S(2)}) %copy-start) | copy-done | bytes 1310744
  2.7 0.0 copy-start.1
  2.7 0.9 %copy-done.1 = bf16[8,64,256]{2,1,0:T(8,128)(2,1)S(1)} copy-done((bf16[8,64,256]{2,1,0:T(8,128)(2,1)S(1)}, bf16[8,64,256]{2,1,0:T(8,128)(2,1)}, u32[]{:S(2)}) %copy-start.1) | copy-done | bytes 262168
  3.7 0.0 copy-start.2
  3.7 0.9 %copy-done.2 = bf16[8,64,256]{2,1,0:T(8,128)(2,1)S(1)} copy-done((bf16[8,64,256]{2,1,0:T(8,128)(2,1)S(1)}, bf16[8,64,256]{2,1,0:T(8,128)(2,1)}, u32[]{:S(2)}) %copy-start.2) | copy-done | bytes 262168
  4.6 0.0 copy-start.3
  4.6 0.9 %copy-done.3 = f32[256,128]{1,0:T(8,128)S(1)} copy-done((f32[256,128]{1,0:T(8,128)S(1)}, f32[256,128]{1,0:T(8,128)}, u32[]{:S(2)}) %copy-start.3) | copy-done | bytes 131096
  5.5 65.1 %shard_map.77 = (f32[2,2,256,128]{3,2,1,0:T(8,128)S(1)}, f32[2,2,128,128]{3,2,1,0:T(8,128)S(1)}, f32[6,2,128,128]{3,2,1,0:T(8,128)S(1)}, f32[5,2,128,128]{3,2,1,0:T(8,128)S(1)}) custom-call(s32[8,5]{1,0:T(8,128)S(1)} %subtract_add_fusion.lidx, bf16[8,5,64,256]{3,2,1,0:T(8,128)(2,1)S(1)} %copy-done, bf16[8,64,256]{2,1,0:T(8,128)(2,1)S(1)} %copy-done.1, ...), custom_call_target="tpu_custom_call" | custom-call | tf_op jit(solution)/shard_map/pallas_call | solution.py:309
  70.7 0.0 copy-done.4
  70.7 13.7 %shard_map.78 = (bf16[2,2,256,128]{3,2,1,0:T(8,128)(2,1)}, bf16[2,1,5,256,128]{4,3,2,1,0:T(8,128)(2,1)}) custom-call(s32[5]{0:T(128)S(1)} %stack.23.bits, s32[6]{0:T(128)S(1)} %copy-done.4, f32[2,2,256,128]{3,2,1,0:T(8,128)S(1)} %get-tuple-element.6.wide, f32[2,2,128,128]{3,2,1,0:T(8,128)S(1)} %get-tuple-element.7.gram, ...), custom_call_target="tpu_custom_call" | custom-call | tf_op jit(solution)/shard_map/pallas_call | solution.py:127
Async XLA Ops:
  0.6 70.1 %copy-start.4 = (s32[6]{0:T(128)S(1)}, s32[6]{0:T(128)}, u32[]{:S(2)}) copy-start(s32[6]{0:T(128)} %ranks.1) | copy-start | bytes 76
  1.4 1.3 %copy-start = (bf16[8,5,64,256]{3,2,1,0:T(8,128)(2,1)S(1)}, bf16[8,5,64,256]{3,2,1,0:T(8,128)(2,1)}, u32[]{:S(2)}) copy-start(bf16[8,5,64,256]{3,2,1,0:T(8,128)(2,1)} %blocks.1) | copy-start | bytes 3932164
  2.7 0.9 %copy-start.1 = (bf16[8,64,256]{2,1,0:T(8,128)(2,1)S(1)}, bf16[8,64,256]{2,1,0:T(8,128)(2,1)}, u32[]{:S(2)}) copy-start(bf16[8,64,256]{2,1,0:T(8,128)(2,1)} %samples.1) | copy-start | bytes 786436
  3.7 0.9 %copy-start.2 = (bf16[8,64,256]{2,1,0:T(8,128)(2,1)S(1)}, bf16[8,64,256]{2,1,0:T(8,128)(2,1)}, u32[]{:S(2)}) copy-start(bf16[8,64,256]{2,1,0:T(8,128)(2,1)} %probes.1) | copy-start | bytes 786436
  4.6 0.9 %copy-start.3 = (f32[256,128]{1,0:T(8,128)S(1)}, f32[256,128]{1,0:T(8,128)}, u32[]{:S(2)}) copy-start(f32[256,128]{1,0:T(8,128)} %compress.1) | copy-start | bytes 393220

commit v3 on v1

v3 whole, which is shorter than its diff:
```python
import math

import jax
import jax.numpy as jnp
from jax import lax
from jax.experimental import pallas as pl
from jax.experimental.pallas import tpu as pltpu
from jax.sharding import PartitionSpec as P

K = 128
F32 = jnp.float32
BF16 = jnp.bfloat16

def pieces(x):
    h = x.astype(BF16).astype(F32)
    r = x - h
    m = r.astype(BF16).astype(F32)
    return h, m, r - m

def panel(S, E, g, p, with_e):
    base = (g * 16 + p) * 64
    rows = [S[pl.ds(base + r, 8, stride=8), :] for r in range(8)]
    erows = [E[pl.ds(base + r, 8, stride=8), :] for r in range(8)] if with_e else None
    a = {}
    for r in range(8):
        for k in range(r, 8):
            c = 8 * p + k
            a[r, k] = jnp.broadcast_to(rows[r][:, c:c + 1], (8, K))
    for r in range(8):
        inv = lax.rsqrt(a[r, r])
        u = {k: a[r, k] * inv for k in range(r + 1, 8)}
        rows[r] = rows[r] * inv
        if with_e:
            erows[r] = erows[r] * inv
        for i in range(r + 1, 8):
            for k in range(i, 8):
                a[i, k] = a[i, k] - u[i] * u[k]
            rows[i] = rows[i] - u[i] * rows[r]
            if with_e:
                erows[i] = erows[i] - u[i] * erows[r]
    for r in range(8):
        S[pl.ds(base + r, 8, stride=8), :] = rows[r]
        if with_e:
            E[pl.ds(base + r, 8, stride=8), :] = erows[r]

def trail(S, E, g, p, b, with_e):
    if p == 15:
        return
    at = lambda q: pl.ds(((g * 16 + q) * 8 + b) * 8, 8)
    h, m, l = pieces(S[at(p), :])
    first = (8 * (p + 1)) // 16 * 16
    left = jnp.concatenate([h, h, h, m, m, l], axis=0).T[first:].astype(BF16)
    right = jnp.concatenate([h, m, l, h, m, h], axis=0)
    if with_e:
        h, m, l = pieces(E[at(p), :])
        right = jnp.concatenate([right, jnp.concatenate([h, m, l, h, m, h], axis=0)], axis=1)
    t = jnp.dot(left, right.astype(BF16), preferred_element_type=F32)
    for q in range(p + 1, 16):
        o = 8 * q - first
        S[at(q), :] = S[at(q), :] - t[o:o + 8, :K]
        if with_e:
            E[at(q), :] = E[at(q), :] - t[o:o + 8, K:]

def get(ref, g, b):
    return jnp.concatenate([ref[pl.ds(((g * 16 + q) * 8 + b) * 8, 8), :] for q in range(16)], axis=0)

def put(ref, g, b, x):
    for q in range(16):
        ref[pl.ds(((g * 16 + q) * 8 + b) * 8, 8), :] = x[8 * q:8 * q + 8]

def cat(x, order):
    h, m, l = x
    d = {"h": h, "m": m, "l": l}
    return jnp.concatenate([d[c] for c in order], axis=1)

def exact_nt(x, y):
    a = cat([v.astype(BF16) for v in pieces(x)], "hhmhml")
    b = cat([v.astype(BF16) for v in pieces(y)], "hmhlmh")
    return lax.dot_general(a, b, (((1,), (1,)), ((), ())), preferred_element_type=F32)


def dot(a, b):
    return jnp.dot(a, b, preferred_element_type=F32)


def dot_nt(a, b):
    return lax.dot_general(a, b, (((1,), (1,)), ((), ())), preferred_element_type=F32)


def halves(x):
    return [v.astype(BF16) for v in pieces(x)]


def remote(src, dst, send, recv, row, col):
    return pltpu.make_async_remote_copy(
        src_ref=src, dst_ref=dst, send_sem=send, recv_sem=recv,
        device_id=(row, col), device_id_type=pl.DeviceIdType.MESH,
    )


def sketch_kernel(
    lidx, ranks, lpad, blocks, samples, probes, compress,
    leaf_out, tr_out,
    S, BL, PR, CM, NB, NP, NL, NS, T1, T3, RO, RI, WS, PO, PI, WO, WI, CH, XG, CG, ZG, FO, FI, WD, GR, CS, CE,
    l_sem, n_sem, xs_send, xs_recv, z_send, z_recv, p_send, p_recv, r_send, r_recv, w_send, w_recv, b_send, b_recv,
):
    row, col = lax.axis_index("row"), lax.axis_index("col")
    rows, cols = lax.axis_size("row"), lax.axis_size("col")
    around = [(row + rows - 1) % rows, (row + 1) % rows]
    peer = [(col + s) % cols for s in range(4)]
    flip = lambda x, n: x + (1 << n) * (1 - 2 * (x // (1 << n) % 2))
    x_mates = [None, flip(col, 0), flip(col, 1), flip(flip(col, 0), 1)]
    z_mates = [None, flip(row, 1), flip(row, 2), flip(flip(row, 1), 2)]
    core_mate = flip(row, 0)

    barrier = pltpu.get_barrier_semaphore()
    greet = [(row, peer[s]) for s in (1, 2, 3)] + [(r, col) for r in around] + [(r, col) for r in z_mates[1:]]
    for device in greet:
        pl.semaphore_signal(barrier, inc=1, device_id=device, device_id_type=pl.DeviceIdType.MESH)
    local = [
        pltpu.make_async_copy(blocks, BL, l_sem.at[0]),
        pltpu.make_async_copy(probes, PR, l_sem.at[1]),
        pltpu.make_async_copy(samples, S.at[:, pl.ds(pl.multiple_of(64 * col, 64), 64)], l_sem.at[2]),
        pltpu.make_async_copy(compress, CM, l_sem.at[3]),
    ]
    for c in local:
        c.start()
    pl.semaphore_wait(barrier, len(greet))

    part = lambda c: pl.ds(pl.multiple_of(64 * c, 64), 64)
    pair = lambda q: pl.ds(2 * q, 2)
    sent = []
    def send(*args):
        c = remote(*args)
        c.start()
        sent.append(c)
        return c
    gather = {s: send(samples, S.at[:, part(col)], xs_send.at[s], xs_recv.at[s], row, peer[s]) for s in (2, 1, 3)}
    near = []
    for n in range(4):
        for d in (0, 1):
            full, crossing = ((0, 1), (4, 3))[d]
            source, target = (
                (lpad, NL.at[1 - d]),
                (blocks.at[:, full], NB.at[1 - d, 0]),
                (blocks.at[:, crossing], NB.at[1 - d, 1]),
                (probes, NP.at[1 - d]),
            )[n]
            near.append(send(source, target, z_send.at[d, n], z_recv.at[1 - d, n], around[d], col))

    def flat(p):
        zt = dot_nt(ct, jnp.concatenate([p, p, p], axis=1))
        return jnp.concatenate(halves(zt), axis=1)
    def term(a, b):
        return dot(a, jnp.concatenate([b, b, b], axis=0))
    one = lambda c: jnp.where(c, 1.0, 0.0).astype(F32)
    for c in local:
        c.wait()
    ch, cm, cl = halves(CM[...])
    ct = jnp.concatenate(halves(CM[...].T), axis=1)
    left = [flat(PR[i]) for i in range(8)]
    for i in range(8):
        T1[i] = term(left[i], BL[i, 1])
        T3[i] = term(left[i], BL[i, 3])
    for j in range(8):
        mid = term(left[j], BL[j, 2])
        for i in range(j + 1, 8):
            mid = mid + one(lidx[i, 1] == 8 + j) * T1[i]
        for i in range(j):
            mid = mid + one(lidx[i, 3] == 8 + j) * T3[i]
        RO[j] = mid

    has = [one(row > 0), one(row < rows - 1)]
    def behind_of(d):
        return (row + rows + 2 * d - 1) % rows
    def arrived(n, d):
        source, target = (
            (lpad, NL.at[d]),
            (blocks.at[:, 0], NB.at[d, 0]),
            (blocks.at[:, 0], NB.at[d, 1]),
            (probes, NP.at[d]),
        )[n]
        remote(source, target, z_send.at[d, n], z_recv.at[d, n], behind_of(d), col).wait_recv()
    def column_of(d, n):
        return NS[d, n, 3 - 2 * d] - 16 * (1 - d)
    def indices(d):
        arrived(0, d)
        copy = pltpu.make_async_copy(NL.at[d], NS.at[d], n_sem.at[d])
        copy.start()
        copy.wait()
    def terms(d):
        exists = jnp.where(d == 0, has[0], has[1])
        left = [flat(NP[d, i]) for i in range(8)]
        for i in range(8):
            T1[i] = exists * term(left[i], NB[d, 1, i])
        for j in range(8):
            total = RO[j] + exists * term(left[j], NB[d, 0, j])
            for i in range(8):
                if i != j:
                    total = total + one(column_of(d, i) == j) * T1[i]
            RO[j] = total
    def products(d):
        for q in range(4):
            acc = []
            for n in (2 * q, 2 * q + 1):
                where = column_of(d, n)
                index = jnp.clip(where, 0, 7)
                acc.append(dot(NB[d, 0, n], S[n]) + one(where == index) * dot(NB[d, 1, n], S[index]))
            PO[d, 2 * q:2 * q + 2] = squeeze(acc)
        send(PO.at[d], PI.at[1 - d], p_send.at[d], p_recv.at[1 - d], behind_of(d), col)
    core = row % 2
    beside, away = 1 - core, core
    for n in (1, 2, 3):
        arrived(n, beside)
    indices(beside)
    terms(beside)
    cc = jnp.concatenate([ch, cm, cl, ch, cm, ch], axis=0)
    def squeeze(acc):
        h, m, l = halves(jnp.concatenate(acc, axis=0))
        return dot(jnp.concatenate([h, h, h, m, m, l], axis=1), cc).reshape(len(acc), 64, K)
    for s in (1, 3, 2):
        gather[s].wait_recv()
    for q in range(4):
        acc = []
        for n in (2 * q, 2 * q + 1):
            behind, ahead = lidx[n, 1], lidx[n, 3]
            total = dot(BL[n, 2], S[n])
            total = total + one(behind >= 8) * dot(BL[n, 1], S[jnp.clip(behind - 8, 0, 7)])
            total = total + one(ahead < 16) * dot(BL[n, 3], S[jnp.clip(ahead - 8, 0, 7)])
            acc.append(total)
        WS[2 * q:2 * q + 2] = squeeze(acc)

    products(beside)
    indices(away)
    for n in (1, 2):
        arrived(n, away)
    products(away)
    arrived(3, away)
    terms(away)
    order = (2, 1, 3)
    reduce = {s: send(RO.at[pair(peer[s])], RI.at[s], r_send.at[s], r_recv.at[s], row, peer[s]) for s in order}

    for d in (0, 1):
        remote(PO.at[d], PI.at[d], p_send.at[d], p_recv.at[d], around[d], col).wait_recv()
    share = {}
    for s in (2, 1, 3, 0):
        q = pair(peer[s])
        w = WS[q] + has[0] * PI[0, q] + has[1] * PI[1, q]
        if s:
            WO[s] = w
            share[s] = send(WO.at[s], WI.at[:, part(col)], w_send.at[s], w_recv.at[s], row, peer[s])
        else:
            WI[:, part(col)] = w

    for s in (1, 3, 2):
        reduce[s].wait_recv()
    for l in range(2):
        vt = RO[2 * col + l] + RI[1, l] + RI[3, l] + RI[2, l]
        WD[1, l] = vt.T
        GR[1, l] = exact_nt(vt, vt)
    for s in (1, 3, 2):
        share[s].wait_recv()
    for l in range(2):
        wt = WI[l].T
        WD[0, l] = WI[l]
        GR[0, l] = exact_nt(wt, wt)

    square = (K, K)
    lane = lax.broadcasted_iota(jnp.int32, square, 1)
    below = lax.broadcasted_iota(jnp.int32, square, 0)
    eye = one(below == lane)
    def factor(groups):
        for g, members in groups:
            for b in range(8):
                put(CS, g, b, members[b][0] if b < len(members) else eye)
                put(CE, g, b, eye)
        for p in range(16):
            for g, members in groups:
                panel(CS, CE, g, p, True)
            for g, members in groups:
                for b, (unused, inverse) in enumerate(members):
                    trail(CS, CE, g, p, b, inverse)
    upper = lambda g, b: jnp.where(below <= lane, get(CS, g, b), 0.0)
    keep = lambda n: jnp.where(lane < ranks[n], math.sqrt(256), 0.0)
    bits = [col % 2, col // 2 % 2, row % 2, row // 2 % 2, row // 4 % 2]
    def merge(j, own, sibling, parent):
        for s in range(2):
            x = get(CE, *parent[s])
            for where, slot in ((bits[j], own[s]), (1 - bits[j], sibling[s])):
                rows_at = pl.ds(pl.multiple_of(where * K, K), K)
                tr_out[s, 0, j, rows_at, :] = (exact_nt(upper(*slot), x) * keep(j + 1)).astype(BF16)

    for side in range(2):
        CH[0, side] = GR[side, 0] + GR[side, 1]
    step = {x: send(CH.at[0], XG.at[x], b_send.at[x], b_recv.at[x], row, x_mates[x]) for x in (2, 3, 1)}
    factor([(0, [(GR[s, l], True) for s in range(2) for l in range(2)] + [(CH[0, s], False) for s in range(2)])])
    for s in range(2):
        for l in range(2):
            x = get(CE, 0, 2 * s + l)
            for half in range(2):
                at = slice(half * K, half * K + K)
                leaf_out[s, l, at, :] = (exact_nt(WD[s, l, at, :], x) * keep(0)).astype(BF16)
    for x in (1, 2, 3):
        step[x].wait_recv()
    first = CH[0] + XG[1]
    second = XG[2] + XG[3]
    CH[1] = first + second
    joined = send(CH.at[1], CG, b_send.at[4], b_recv.at[4], core_mate, col)
    joined.wait_recv()
    third = CG[...]
    CH[2] = CH[1] + third
    mine, other = row % 2, 1 - row % 2
    step = {x: send(CH.at[2, mine], ZG.at[x], b_send.at[4 + x], b_recv.at[4 + x], z_mates[x], col) for x in (3, 2, 1)}
    factor([
        (1, [(XG[1, s], False) for s in range(2)] + [(second[s], False) for s in range(2)]
            + [(first[s], True) for s in range(2)] + [(CH[1, s], True) for s in range(2)]),
        (2, [(third[s], False) for s in range(2)] + [(CH[2, s], True) for s in range(2)]),
    ])
    for x in (1, 2, 3):
        step[x].wait_recv()
    FO[0] = ZG[1]
    FO[1] = ZG[2] + ZG[3]
    last = send(FO, FI, b_send.at[0], b_recv.at[0], core_mate, col)
    merge(0, [(0, 4), (0, 5)], [(1, 0), (1, 1)], [(1, 4), (1, 5)])
    merge(1, [(1, 4), (1, 5)], [(1, 2), (1, 3)], [(1, 6), (1, 7)])
    merge(2, [(1, 6), (1, 7)], [(2, 0), (2, 1)], [(2, 2), (2, 3)])
    last.wait_recv()
    swap = row % 2 == 1
    fourth = [jnp.where(swap, FI[0], FO[0]), jnp.where(swap, FO[0], FI[0])]
    fifth = [jnp.where(swap, FI[1], FO[1]), jnp.where(swap, FO[1], FI[1])]
    level = [CH[2, s] + fourth[s] for s in range(2)]
    factor([(3, [(v, False) for v in fourth + fifth] + [(v, True) for v in level] + [(level[s] + fifth[s], True) for s in range(2)])])
    merge(3, [(2, 2), (2, 3)], [(3, 0), (3, 1)], [(3, 4), (3, 5)])
    merge(4, [(3, 4), (3, 5)], [(3, 2), (3, 3)], [(3, 6), (3, 7)])
    for c in sent:
        c.wait_send()


def sketch(lidx, ranks, lpad, blocks, samples, probes, compress):
    vm = pl.BlockSpec(memory_space=pltpu.VMEM)
    sm = pl.BlockSpec(memory_space=pltpu.SMEM)
    hbm = pl.BlockSpec(memory_space=pltpu.HBM)
    dma = pltpu.SemaphoreType.DMA
    shape = jax.ShapeDtypeStruct
    return pl.pallas_call(
        sketch_kernel,
        out_shape=(
            shape((2, 2, 256, K), BF16), shape((2, 1, 5, 256, K), BF16),
        ),
        in_specs=[sm, sm, vm, hbm, hbm, hbm, hbm],
        out_specs=(vm, vm),
        scratch_shapes=[
            pltpu.VMEM((8, 256, 256), BF16),
            pltpu.VMEM((8, 5, 64, 256), BF16), pltpu.VMEM((8, 64, 256), BF16), pltpu.VMEM((256, K), F32),
            pltpu.VMEM((2, 2, 8, 64, 256), BF16), pltpu.VMEM((2, 8, 64, 256), BF16),
            pltpu.VMEM((2, 8, K), jnp.int32), pltpu.SMEM((2, 8, K), jnp.int32),
            pltpu.VMEM((8, K, 256), F32), pltpu.VMEM((8, K, 256), F32),
            pltpu.VMEM((8, K, 256), F32), pltpu.VMEM((4, 2, K, 256), F32),
            pltpu.VMEM((8, 64, K), F32), pltpu.VMEM((2, 8, 64, K), F32), pltpu.VMEM((2, 8, 64, K), F32),
            pltpu.VMEM((4, 2, 64, K), F32), pltpu.VMEM((2, 256, K), F32),
            pltpu.VMEM((3, 2, K, K), F32), pltpu.VMEM((4, 2, K, K), F32), pltpu.VMEM((2, K, K), F32),
            pltpu.VMEM((4, K, K), F32), pltpu.VMEM((2, K, K), F32), pltpu.VMEM((2, K, K), F32),
            pltpu.VMEM((2, 2, 256, K), F32), pltpu.VMEM((2, 2, K, K), F32),
            pltpu.VMEM((4096, K), F32), pltpu.VMEM((4096, K), F32),
            dma((4,)), dma((2,)), dma((4,)), dma((4,)), dma((2, 4)), dma((2, 4)), dma((2,)), dma((2,)),
            dma((4,)), dma((4,)), dma((4,)), dma((4,)), dma((8,)), dma((8,)),
        ],
        compiler_params=pltpu.CompilerParams(
            collective_id=0, has_side_effects=True, vmem_limit_bytes=60 << 20
        ),
    )(lidx, ranks, lpad, blocks, samples, probes, compress)


def body(blocks, samples, probes, compress, pattern, ranks):
    n_blocks = blocks.shape[0]
    local_index = pattern - lax.axis_index("row") * n_blocks + n_blocks
    padded_index = jnp.pad(local_index, ((0, 0), (0, compress.shape[1] - local_index.shape[1])))
    return sketch(local_index, ranks, padded_index, blocks, samples, probes, compress)


def solution(mesh):
    return jax.shard_map(
        body,
        mesh=mesh,
        in_specs=(
            P("row", None, "col", None),
            P("row", "col", None),
            P("row", "col", None),
            P(),
            P("row", None),
            P(),
        ),
        out_specs=(P(None, ("row", "col"), None, None), P(None, ("row", "col"), None, None, None)),
        check_vma=False,
    )
```

time: 200 us -> 77 us (0.39)
  waiting for transfers between devices: 61.8 us -> 0 us
  Pallas kernels: 13.5 us -> 71.2 us
  starting transfers between devices: 33.7 us -> 0 us
  other arithmetic: 28.8 us -> 0.69 us
  matrix products: 17.1 us -> 0 us
  local copies, waits for them, and re-layouts: 18 us -> 4.24 us
  between operations: 14.4 us -> 0.65 us
  blocking collectives: 12 us -> 0 us
    pallas_call x1, Pallas kernels: 13.5 us -> 71.2 us  [sketch(): pl.pallas_call(sketch_kernel, out_shape=(shape((2, 2, 256, K), BF16), sha...]
    ppermute x9 -> x0, waiting for transfers between devices: 55.2 us -> none  [the longest x2 22.4 us: passed_along(): return lax.ppermute(value, axis, pairs)]
    ppermute x9 -> x0, starting transfers between devices: 33.6 us -> none  [the longest x5 16.7 us: partner(): lax.ppermute(value, axis, [(i, i ^ 1 << distance) for i in range(lax.axis...]
    scatter-add x5 -> x0, other arithmetic: 24.5 us -> none  [body(): buffer = buffer.at[local_index[:, slot]].add(term)]
    dot_general x12 -> x0, matrix products: 17.1 us -> none  [the longest x5 9.69 us: body(): jnp.einsum('nrc,nrs->ncs', blocks[:, slot], probes, preferred_element_typ...]
    all_to_all x1 -> x0, blocking collectives: 12 us -> none  [body(): lax.all_to_all(partial_value, 'col', split_axis=0, concat_axis=1, tiled=T...]
    gather x5 -> x0, local copies, waits for them, and re-layouts: 8.03 us -> none  [body(): picked = extended[local_index[:, slot]]]
    all_gather x1 -> x0, waiting for transfers between devices: 6.61 us -> none  [body(): full_rows = lax.all_gather(samples, 'col', axis=1, tiled=True)]
  transfers between devices with their start and end apart: 11 -> 0, of which waited for: 10 -> 0; matrix products, arithmetic and copies ran while one was open for 8% -> 0% of each run, Pallas kernels for 0% -> 0%
where the time goes in v3:
time: 77 us; the launch traced here: 76.8 us
  Pallas kernels  71.2 us (92%)
  local copies, waits for them, and re-layouts  4.24 us (6%)
    pallas_call x1, Pallas kernels, sketch(): pl.pallas_call(sketch_kernel, out_shape=(shape((2, 2, 256, K), BF16), sha...  71.2 us
    unnamed x4, local copies, waits for them, and re-layouts  3.65 us

profile of v3, /device:TPU:1, one launch (start us, length us, event | category | flops | bytes accessed | tf_op | source)
XLA Modules:
  0.0 76.8 jit_solution(4375859848649881811)
XLA Ops:
  0.6 0.7 subtract_add_fusion.lidx
  1.3 0.0 copy-start
  1.3 0.6 pad.4.lpad
  1.9 0.0 copy-done
  1.9 71.2 %shard_map.77 = (bf16[2,2,256,128]{3,2,1,0:T(8,128)(2,1)}, bf16[2,1,5,256,128]{4,3,2,1,0:T(8,128)(2,1)}) custom-call(s32[8,5]{1,0:T(8,128)} %copy-done, s32[6]{0:T(128)} %ranks.1, s32[8,128]{1,0:T(8,128)} %pad.4.lpad, bf16[8,5,64,256]{3,2,1,0:T(8,128)(2,1)} %blocks.1, bf16[8,64,256]{2,1,0:T(8,128)(2,1)} %samples.1, bf16[8,64,256]{2,1,0:T(8,128)(2,1)} %probes.1, ...), custom_call_target="tpu_custom_call" | custom-call | tf_op jit(solution)/shard_map/pallas_call | solution.py:345
  73.1 1.7 %copy.10 = bf16[2,2,256,128]{3,2,1,0:T(8,128)(2,1)} copy(bf16[2,2,256,128]{3,2,1,0:T(8,128)(2,1)} %get-tuple-element.4) | data formatting | bytes 524288
  74.8 2.0 %copy.11 = bf16[2,1,5,256,128]{4,3,2,1,0:T(8,128)(2,1)} copy(bf16[2,1,5,256,128]{4,3,2,1,0:T(8,128)(2,1)} %get-tuple-element.5) | data formatting | bytes 1310720
Async XLA Ops:
  1.3 0.6 copy-start

commit v4 on v3

--- a/solution.py
+++ b/solution.py
@@ -99,9 +99,9 @@
 
 
 def sketch_kernel(
-    lidx, ranks, lpad, blocks, samples, probes, compress,
+    pattern, ranks, names, blocks, samples, probes, compress,
     leaf_out, tr_out,
-    S, BL, PR, CM, NB, NP, NL, NS, T1, T3, RO, RI, WS, PO, PI, WO, WI, CH, XG, CG, ZG, FO, FI, WD, GR, CS, CE,
+    S, BL, PR, CM, LP, NB, NP, NL, NS, T1, T3, RO, RI, WS, PO, PI, WO, WI, CH, XG, CG, ZG, FO, FI, WD, GR, CS, CE,
     l_sem, n_sem, xs_send, xs_recv, z_send, z_recv, p_send, p_recv, r_send, r_recv, w_send, w_recv, b_send, b_recv,
 ):
     row, col = lax.axis_index("row"), lax.axis_index("col")
@@ -112,6 +112,8 @@
     x_mates = [None, flip(col, 0), flip(col, 1), flip(flip(col, 0), 1)]
     z_mates = [None, flip(row, 1), flip(row, 2), flip(flip(row, 1), 2)]
     core_mate = flip(row, 0)
+
+    base = 8 * row
 
     barrier = pltpu.get_barrier_semaphore()
     greet = [(row, peer[s]) for s in (1, 2, 3)] + [(r, col) for r in around] + [(r, col) for r in z_mates[1:]]
@@ -125,6 +127,8 @@
     ]
     for c in local:
         c.start()
+    LP[...] = jnp.zeros_like(LP)
+    LP[:, :5] = names[...]
     pl.semaphore_wait(barrier, len(greet))
 
     part = lambda c: pl.ds(pl.multiple_of(64 * c, 64), 64)
@@ -136,17 +140,18 @@
         sent.append(c)
         return c
     gather = {s: send(samples, S.at[:, part(col)], xs_send.at[s], xs_recv.at[s], row, peer[s]) for s in (2, 1, 3)}
-    near = []
-    for n in range(4):
+    def to_neighbours(n):
         for d in (0, 1):
             full, crossing = ((0, 1), (4, 3))[d]
             source, target = (
-                (lpad, NL.at[1 - d]),
+                (LP, NL.at[1 - d]),
                 (blocks.at[:, full], NB.at[1 - d, 0]),
                 (blocks.at[:, crossing], NB.at[1 - d, 1]),
                 (probes, NP.at[1 - d]),
             )[n]
-            near.append(send(source, target, z_send.at[d, n], z_recv.at[1 - d, n], around[d], col))
+            send(source, target, z_send.at[d, n], z_recv.at[1 - d, n], around[d], col)
+    for n in range(3):
+        to_neighbours(n)
 
     def flat(p):
         zt = dot_nt(ct, jnp.concatenate([p, p, p], axis=1))
@@ -165,24 +170,26 @@
     for j in range(8):
         mid = term(left[j], BL[j, 2])
         for i in range(j + 1, 8):
-            mid = mid + one(lidx[i, 1] == 8 + j) * T1[i]
+            mid = mid + one(pattern[i, 1] - base == j) * T1[i]
         for i in range(j):
-            mid = mid + one(lidx[i, 3] == 8 + j) * T3[i]
+            mid = mid + one(pattern[i, 3] - base == j) * T3[i]
         RO[j] = mid
+        if j == 0:
+            to_neighbours(3)
 
     has = [one(row > 0), one(row < rows - 1)]
     def behind_of(d):
         return (row + rows + 2 * d - 1) % rows
     def arrived(n, d):
         source, target = (
-            (lpad, NL.at[d]),
+            (LP, NL.at[d]),
             (blocks.at[:, 0], NB.at[d, 0]),
             (blocks.at[:, 0], NB.at[d, 1]),
             (probes, NP.at[d]),
         )[n]
         remote(source, target, z_send.at[d, n], z_recv.at[d, n], behind_of(d), col).wait_recv()
     def column_of(d, n):
-        return NS[d, n, 3 - 2 * d] - 16 * (1 - d)
+        return NS[d, n, 3 - 2 * d] - base
     def indices(d):
         arrived(0, d)
         copy = pltpu.make_async_copy(NL.at[d], NS.at[d], n_sem.at[d])
@@ -207,7 +214,7 @@
                 index = jnp.clip(where, 0, 7)
                 acc.append(dot(NB[d, 0, n], S[n]) + one(where == index) * dot(NB[d, 1, n], S[index]))
             PO[d, 2 * q:2 * q + 2] = squeeze(acc)
-        send(PO.at[d], PI.at[1 - d], p_send.at[d], p_recv.at[1 - d], behind_of(d), col)
+            send(PO.at[d, pair(q)], PI.at[1 - d, pair(q)], p_send.at[d, q], p_recv.at[1 - d, q], behind_of(d), col)
     core = row % 2
     beside, away = 1 - core, core
     for n in (1, 2, 3):
@@ -223,10 +230,11 @@
     for q in range(4):
         acc = []
         for n in (2 * q, 2 * q + 1):
-            behind, ahead = lidx[n, 1], lidx[n, 3]
             total = dot(BL[n, 2], S[n])
-            total = total + one(behind >= 8) * dot(BL[n, 1], S[jnp.clip(behind - 8, 0, 7)])
-            total = total + one(ahead < 16) * dot(BL[n, 3], S[jnp.clip(ahead - 8, 0, 7)])
+            for k in (1, 3):
+                where = pattern[n, k] - base
+                index = jnp.clip(where, 0, 7)
+                total = total + one(where == index) * dot(BL[n, k], S[index])
             acc.append(total)
         WS[2 * q:2 * q + 2] = squeeze(acc)
 
@@ -240,11 +248,11 @@
     order = (2, 1, 3)
     reduce = {s: send(RO.at[pair(peer[s])], RI.at[s], r_send.at[s], r_recv.at[s], row, peer[s]) for s in order}
 
-    for d in (0, 1):
-        remote(PO.at[d], PI.at[d], p_send.at[d], p_recv.at[d], around[d], col).wait_recv()
     share = {}
     for s in (2, 1, 3, 0):
         q = pair(peer[s])
+        for d in (0, 1):
+            remote(PO.at[d, q], PI.at[d, q], p_send.at[d, peer[s]], p_recv.at[d, peer[s]], around[d], col).wait_recv()
         w = WS[q] + has[0] * PI[0, q] + has[1] * PI[1, q]
         if s:
             WO[s] = w
@@ -294,18 +302,18 @@
         CH[0, side] = GR[side, 0] + GR[side, 1]
     step = {x: send(CH.at[0], XG.at[x], b_send.at[x], b_recv.at[x], row, x_mates[x]) for x in (2, 3, 1)}
     factor([(0, [(GR[s, l], True) for s in range(2) for l in range(2)] + [(CH[0, s], False) for s in range(2)])])
+    for x in (1, 2, 3):
+        step[x].wait_recv()
+    first = CH[0] + XG[1]
+    second = XG[2] + XG[3]
+    CH[1] = first + second
+    joined = send(CH.at[1], CG, b_send.at[4], b_recv.at[4], core_mate, col)
     for s in range(2):
         for l in range(2):
             x = get(CE, 0, 2 * s + l)
             for half in range(2):
                 at = slice(half * K, half * K + K)
                 leaf_out[s, l, at, :] = (exact_nt(WD[s, l, at, :], x) * keep(0)).astype(BF16)
-    for x in (1, 2, 3):
-        step[x].wait_recv()
-    first = CH[0] + XG[1]
-    second = XG[2] + XG[3]
-    CH[1] = first + second
-    joined = send(CH.at[1], CG, b_send.at[4], b_recv.at[4], core_mate, col)
     joined.wait_recv()
     third = CG[...]
     CH[2] = CH[1] + third
@@ -336,7 +344,7 @@
         c.wait_send()
 
 
-def sketch(lidx, ranks, lpad, blocks, samples, probes, compress):
+def sketch(pattern, ranks, blocks, samples, probes, compress):
     vm = pl.BlockSpec(memory_space=pltpu.VMEM)
     sm = pl.BlockSpec(memory_space=pltpu.SMEM)
     hbm = pl.BlockSpec(memory_space=pltpu.HBM)
@@ -351,7 +359,7 @@
         out_specs=(vm, vm),
         scratch_shapes=[
             pltpu.VMEM((8, 256, 256), BF16),
-            pltpu.VMEM((8, 5, 64, 256), BF16), pltpu.VMEM((8, 64, 256), BF16), pltpu.VMEM((256, K), F32),
+            pltpu.VMEM((8, 5, 64, 256), BF16), pltpu.VMEM((8, 64, 256), BF16), pltpu.VMEM((256, K), F32), pltpu.VMEM((8, K), jnp.int32),
             pltpu.VMEM((2, 2, 8, 64, 256), BF16), pltpu.VMEM((2, 8, 64, 256), BF16),
             pltpu.VMEM((2, 8, K), jnp.int32), pltpu.SMEM((2, 8, K), jnp.int32),
             pltpu.VMEM((8, K, 256), F32), pltpu.VMEM((8, K, 256), F32),
@@ -362,20 +370,17 @@
             pltpu.VMEM((4, K, K), F32), pltpu.VMEM((2, K, K), F32), pltpu.VMEM((2, K, K), F32),
             pltpu.VMEM((2, 2, 256, K), F32), pltpu.VMEM((2, 2, K, K), F32),
             pltpu.VMEM((4096, K), F32), pltpu.VMEM((4096, K), F32),
-            dma((4,)), dma((2,)), dma((4,)), dma((4,)), dma((2, 4)), dma((2, 4)), dma((2,)), dma((2,)),
+            dma((4,)), dma((2,)), dma((4,)), dma((4,)), dma((2, 4)), dma((2, 4)), dma((2, 4)), dma((2, 4)),
             dma((4,)), dma((4,)), dma((4,)), dma((4,)), dma((8,)), dma((8,)),
         ],
         compiler_params=pltpu.CompilerParams(
             collective_id=0, has_side_effects=True, vmem_limit_bytes=60 << 20
         ),
-    )(lidx, ranks, lpad, blocks, samples, probes, compress)
+    )(pattern, ranks, pattern, blocks, samples, probes, compress)
 
 
 def body(blocks, samples, probes, compress, pattern, ranks):
-    n_blocks = blocks.shape[0]
-    local_index = pattern - lax.axis_index("row") * n_blocks + n_blocks
-    padded_index = jnp.pad(local_index, ((0, 0), (0, compress.shape[1] - local_index.shape[1])))
-    return sketch(local_index, ranks, padded_index, blocks, samples, probes, compress)
+    return sketch(pattern, ranks, blocks, samples, probes, compress)
 
 
 def solution(mesh):

time: 77 us -> 76.6 us (level)
  Pallas kernels: 71.2 us -> 72.1 us
    pallas_call x1, Pallas kernels: 71.2 us -> 72.1 us  [sketch(): pl.pallas_call(sketch_kernel, out_shape=(shape((2, 2, 256, K), BF16), sha...]
    unnamed x4 -> x2, local copies, waits for them, and re-layouts: 3.65 us -> 3.64 us
where the time goes in v4:
time: 76.6 us; the launch traced here: 76.3 us
  Pallas kernels  72.1 us (94%)
  local copies, waits for them, and re-layouts  3.64 us (5%)
    pallas_call x1, Pallas kernels, sketch(): pl.pallas_call(sketch_kernel, out_shape=(shape((2, 2, 256, K), BF16), sha...  72.1 us
    unnamed x2, local copies, waits for them, and re-layouts  3.64 us

profile of v4, /device:TPU:1, one launch (start us, length us, event | category | flops | bytes accessed | tf_op | source)
XLA Modules:
  0.0 76.3 jit_solution(17984105917684344201)
XLA Ops:
  0.6 72.1 %shard_map.77 = (bf16[2,2,256,128]{3,2,1,0:T(8,128)(2,1)}, bf16[2,1,5,256,128]{4,3,2,1,0:T(8,128)(2,1)}) custom-call(s32[8,5]{1,0:T(8,128)} %names.1, s32[6]{0:T(128)} %ranks.1, s32[8,5]{1,0:T(8,128)} %names.1, bf16[8,5,64,256]{3,2,1,0:T(8,128)(2,1)} %blocks.1, bf16[8,64,256]{2,1,0:T(8,128)(2,1)} %samples.1, bf16[8,64,256]{2,1,0:T(8,128)(2,1)} %probes.1, ...), custom_call_target="tpu_custom_call" | custom-call | tf_op jit(solution)/shard_map/pallas_call | solution.py:353
  72.7 1.7 %copy.10 = bf16[2,2,256,128]{3,2,1,0:T(8,128)(2,1)} copy(bf16[2,2,256,128]{3,2,1,0:T(8,128)(2,1)} %get-tuple-element.4) | data formatting | bytes 524288
  74.4 2.0 %copy.11 = bf16[2,1,5,256,128]{4,3,2,1,0:T(8,128)(2,1)} copy(bf16[2,1,5,256,128]{4,3,2,1,0:T(8,128)(2,1)} %get-tuple-element.5) | data formatting | bytes 1310720
